TPU v7x, 32 devices: a whole 2x2x4 slice. The times are simulated.
32 devices in a mesh: group: 2 (over y), shard: 16 (over z, x, core).
Axes of the slice: x: 2, y: 2, z: 4, core: 2. Of those that a mesh axis runs over, the one named last changes fastest.
Arguments:
- item_features: bfloat16 [4096, 1024], P(('group', 'shard')), may hold values from -6 to 6
- tower_weight: bfloat16 [1024, 1024], replicated, may hold values from -0.1875 to 0.1875
- item_table: bfloat16 [4096, 1024], P(('group', 'shard')), may hold values from -4 to 4
- owner: int32 [4096, 1], P(('group', 'shard')), may hold values from 0 to 15; in each aligned block of 128 rows (0 to 127, 128 to 255, ...) at most 16 rows name the same one
- table_slot: int32 [4096], P(('group', 'shard')), may hold values from 0 to 127
- pair_users: int32 [4096, 2], P(('group', 'shard')), may hold values from 0 to 63
- user_comps: bfloat16 [128, 1024], P(('group', 'shard')), may hold values from -0.5 to 0.5
- user_gates: bfloat16 [128, 64], P(('group', 'shard')), may hold values from -6 to 6
Outputs:
- tower_grad: float32 [1024, 1024], P('shard')
- table_grad: float32 [4096, 1024], P(('group', 'shard'))
- user_comp_grad: float32 [128, 1024], P(('group', 'shard'))
- user_gate_grad: float32 [128, 64], P(('group', 'shard'))
Inputs may be any that keep to these rules, and one draw needn't show every extreme that they name: Among the rows of one device, no owner is named more than 16 times, a bound that some block reaches. `pair_users`: user numbers within the item's own group.
All inputs are finite; a program needn't handle non-finite values.
Results may differ from a plain program's by a relative error of at most 0.0042.
Values may be sent and summed in bfloat16 or wider, within the bound.
No kernel may reach another device: no remote copies, remote signals or barrier semaphores. Data moves between devices by JAX's collectives and lax.ppermute only.
A program may use at most 64 MiB of HBM per device.

v0:
```python
import jax
import jax.numpy as jnp
from jax import lax
from jax.sharding import PartitionSpec as P

COMPS = 8


highest = lax.Precision.HIGHEST


def exact_gelu(values):
    return jax.nn.gelu(values, approximate=False)


def mixture_score(normed, users, gates):
    rows_here = normed.shape[0]
    logits = jnp.einsum("npk,nqk->npq", users, normed, precision=highest)
    weights = jax.nn.sigmoid(gates.reshape(rows_here, COMPS, COMPS) + logits)
    return 0.125 * jnp.sum(weights * logits, axis=(1, 2))


def pair_loss(embedded, table_rows, pos_users, neg_users, pos_gates, neg_gates, present):
    rows_here = embedded.shape[0]
    combined = (embedded + table_rows).reshape(rows_here, COMPS, -1)
    normed = combined * lax.rsqrt(jnp.mean(combined * combined, axis=-1, keepdims=True) + 1e-06)
    pos_score = mixture_score(normed, pos_users.reshape(rows_here, COMPS, -1), pos_gates)
    neg_score = mixture_score(normed, neg_users.reshape(rows_here, COMPS, -1), neg_gates)
    return jnp.sum(present * (jax.nn.softplus(-pos_score) + jax.nn.softplus(neg_score)))


def pick_rows(selector, table):
    return jnp.dot(selector, table, preferred_element_type=jnp.float32)


def spread_back(index, values, row_total):
    return jnp.zeros((row_total, values.shape[1]), jnp.float32).at[index].add(values)


def local(
    item_features, tower_weight, item_table, owner, table_slot, pair_users, user_comps, user_gates
):
    shards = lax.axis_size("shard")
    item_count = item_features.shape[0]
    capacity = max(2, 2 * item_count // shards)
    buffer_rows = shards * capacity
    preact = jnp.dot(item_features, tower_weight, preferred_element_type=jnp.float32)
    gelu_value, gelu_back = jax.vjp(exact_gelu, preact)
    embedded = gelu_value.astype(jnp.bfloat16)
    target = owner[:, 0]
    onehot = (target[:, None] == jnp.arange(shards, dtype=jnp.int32)[None, :]).astype(jnp.bfloat16)
    item_ids = jnp.arange(item_count, dtype=jnp.int32)
    earlier = (item_ids[:, None] > item_ids[None, :]).astype(jnp.bfloat16)
    before = jnp.dot(earlier, onehot, preferred_element_type=jnp.float32)
    within = jnp.sum(before * onehot.astype(jnp.float32), axis=1).astype(jnp.int32)
    position = target * capacity + within
    source = jnp.zeros((buffer_rows,), jnp.int32).at[position].set(item_ids)
    filled = jnp.zeros((buffer_rows,), jnp.int32).at[position].set(1)
    send_rows = jnp.where(filled[:, None] > 0, embedded[source], jnp.zeros((), jnp.bfloat16))
    headers = jnp.stack(
        [table_slot[source], pair_users[source, 0], pair_users[source, 1], filled], axis=1
    )
    headers = headers * filled[:, None]
    got_rows, got_headers = (
        lax.all_to_all(send_rows, "shard", split_axis=0, concat_axis=0, tiled=True),
        lax.all_to_all(headers, "shard", split_axis=0, concat_axis=0, tiled=True),
    )
    all_users, all_gates = (
        lax.all_gather(user_comps, "shard", axis=0, tiled=True),
        lax.all_gather(user_gates, "shard", axis=0, tiled=True),
    )
    table_ids = jnp.arange(item_table.shape[0], dtype=jnp.int32)
    user_ids = jnp.arange(all_users.shape[0], dtype=jnp.int32)
    pick_table = (got_headers[:, 0:1] == table_ids[None, :]).astype(jnp.bfloat16)
    pick_pos = (got_headers[:, 1:2] == user_ids[None, :]).astype(jnp.bfloat16)
    pick_neg = (got_headers[:, 2:3] == user_ids[None, :]).astype(jnp.bfloat16)
    present = got_headers[:, 3].astype(jnp.float32)
    table_rows = pick_rows(pick_table, item_table)
    pos_users = pick_rows(pick_pos, all_users)
    neg_users = pick_rows(pick_neg, all_users)
    pos_gates = pick_rows(pick_pos, all_gates)
    neg_gates = pick_rows(pick_neg, all_gates)
    derivs = jax.grad(pair_loss, argnums=(0, 1, 2, 3, 4, 5))(
        got_rows.astype(jnp.float32),
        table_rows,
        pos_users,
        neg_users,
        pos_gates,
        neg_gates,
        present,
    )
    table_total = item_table.shape[0]
    user_total = all_users.shape[0]
    table_grad = spread_back(got_headers[:, 0], derivs[1], table_total)
    user_partial = spread_back(got_headers[:, 1], derivs[2], user_total) + spread_back(
        got_headers[:, 2], derivs[3], user_total
    )
    gate_partial = spread_back(got_headers[:, 1], derivs[4], user_total) + spread_back(
        got_headers[:, 2], derivs[5], user_total
    )
    returned = lax.all_to_all(
        derivs[0].astype(jnp.bfloat16), "shard", split_axis=0, concat_axis=0, tiled=True
    )
    own_rows = returned[position]
    d_preact = gelu_back(own_rows.astype(jnp.float32))[0].astype(jnp.bfloat16)
    partial_value = lax.psum_scatter(
        lax.dot_general(
            item_features, d_preact, (((0,), (0,)), ((), ())), preferred_element_type=jnp.float32
        ),
        "shard",
        scatter_dimension=0,
        tiled=True,
    )
    tower_grad = lax.psum(partial_value, "group")
    got_users, got_gates = (
        lax.all_to_all(user_partial, "shard", split_axis=0, concat_axis=0, tiled=True),
        lax.all_to_all(gate_partial, "shard", split_axis=0, concat_axis=0, tiled=True),
    )
    held = user_comps.shape[0]
    user_comp_grad = jnp.sum(got_users.reshape(shards, held, -1), axis=0)
    user_gate_grad = jnp.sum(got_gates.reshape(shards, held, -1), axis=0)
    return (tower_grad, table_grad, user_comp_grad, user_gate_grad)


def solution(mesh):
    placed = (
        P(("group", "shard"), None),
        P(),
        P(("group", "shard"), None),
        P(("group", "shard"), None),
        P(("group", "shard")),
        P(("group", "shard"), None),
        P(("group", "shard"), None),
        P(("group", "shard"), None),
    )
    return jax.shard_map(
        local,
        mesh=mesh,
        in_specs=placed,
        out_specs=(
            P("shard", None),
            P(("group", "shard"), None),
            P(("group", "shard"), None),
            P(("group", "shard"), None),
        ),
        check_vma=False,
    )
```

profile of v0, /device:TPU:0, one launch (start us, length us, event | category | flops | bytes accessed | tf_op | source)
XLA Modules:
  0.0 257.6 jit_solution(18045161025202038954)
XLA Ops:
  18.4 7.4 %all-to-all-start = ((s32[16,16,4]{1,2,0:T(4,128)}), s32[16,16,4]{1,2,0:T(4,128)S(1)}, u32[]{:S(2)}, u32[]{:S(2)}) async-start(s32[16,16,4]{1,2,0:T(4,128)} %copy.95), calls=%async_computation | async-start | bytes 65536 | tf_op jit(solution)/shard_map/all_to_all | solution.py:66
  30.1 2.3 all-to-all-done
  32.4 3.7 %all-to-all-start.1 = ((bf16[16,16,1024]{2,1,0:T(8,128)(2,1)}), bf16[16,16,1024]{2,1,0:T(8,128)(2,1)S(1)}, u32[]{:S(2)}, u32[]{:S(2)}) async-start(bf16[16,16,1024]{2,1,0:T(8,128)(2,1)} %broadcast_select_fusion), calls=%async_computation.1 | async-start | bytes 1048576 | tf_op jit(solution)/shard_map/all_to_all | solution.py:65
  36.1 25.4 %all-gather.1 = bf16[16,4,1024]{2,1,0:T(4,128)(2,1)S(1)} all-gather(bf16[1,4,1024]{2,1,0:T(4,128)(2,1)S(1)} %bitcast.114), channel_id=1, replica_groups=mesh['group'=2,'shard'=16] {'shard'}, dimensions={0}, use_global_device_ids=true | all-gather | bytes 139264 | tf_op jit(solution)/shard_map/all_gather | solution.py:69
  61.5 19.0 %all-gather = bf16[16,4,64]{2,1,0:T(4,128)(2,1)S(1)} all-gather(bf16[1,4,64]{2,1,0:T(4,128)(2,1)S(1)} %bitcast.121), channel_id=1, replica_groups=mesh['group'=2,'shard'=16] {'shard'}, dimensions={0}, use_global_device_ids=true | all-gather | bytes 8704 | tf_op jit(solution)/shard_map/all_gather | solution.py:70
  85.4 4.1 %fusion.27 = f32[256,8,8]{2,1,0:T(8,128)} fusion(f32[256,8,128]{2,1,0:T(8,128)} %bitcast.102, f32[256,8,128]{2,1,0:T(8,128)S(1)} %bitcast.97, f32[256,8]{1,0:T(8,128)S(1)} %copy.98), kind=kOutput, calls=%fused_computation.50 | convolution fusion | flops 25427968 | bytes 2170880 | tf_op jit(solution)/shard_map/jvp(npk,nqk->npq)/dot_general | solution.py:18
  91.0 4.1 %fusion.25 = f32[256,8,8]{2,1,0:T(8,128)} fusion(f32[256,8,128]{2,1,0:T(8,128)} %bitcast.104, f32[256,8,128]{2,1,0:T(8,128)S(1)} %bitcast.98, f32[256,8]{1,0:T(8,128)S(1)} %copy.98), kind=kOutput, calls=%fused_computation.48 | convolution fusion | flops 25427968 | bytes 2170880 | tf_op jit(solution)/shard_map/jvp(npk,nqk->npq)/dot_general | solution.py:18
  100.5 3.9 %fusion.86 = f32[256,8,128]{2,1,0:T(8,128)S(1)} fusion(f32[256,8,8]{2,1,0:T(8,128)} %copy.110, f32[256,8,128]{2,1,0:T(8,128)} %bitcast.103), kind=kOutput, calls=%fused_computation.153 | convolution fusion | flops 25165824 | bytes 2162688 | tf_op jit(solution)/shard_map/transpose(jvp(npk,nqk->npq))/dot_general | solution.py:18
  104.5 3.3 %multiply_reduce_fusion = (f32[256,8]{1,0:T(8,128)S(1)}, f32[256,8,128]{2,1,0:T(8,128)}) fusion(f32[256,8,128]{2,1,0:T(8,128)S(1)} %bitcast.99, f32[256,8,128]{2,1,0:T(8,128)S(1)} %fusion.86, f32[256,8,8]{2,1,0:T(8,128)S(1)} %copy-done.3, f32[256,8,128]{2,1,0:T(8,128)S(1)} %bitcast.105), kind=kOutput, calls=%fused_computation.42 | convolution fusion | flops 25950208 | bytes 4268032 | tf_op jit(solution)/shard_map/transpose(jvp(npk,nqk->npq))/dot_general | solution.py:18
  108.0 2.9 %fusion.85 = (bf16[256,8,128]{2,1,0:T(8,128)(2,1)}, f32[256,8,128]{2,1,0:T(8,128)}) fusion(f32[256,8]{1,0:T(8,128)S(1)} %copy.108, f32[32,8,8,128]{3,2,1,0:T(8,128)S(1)} %copy.119, f32[256,8,128]{2,1,0:T(8,128)} %get-tuple-element.65, f32[256,8]{1,0:T(8,128)S(1)} %copy.98), kind=kLoop, calls=%fused_computation.152 | loop fusion | flops 1310720 | bytes 3686400 | tf_op jit(solution)/shard_map/convert_element_type | solution.py:102
  113.0 4.2 %all-to-all-start.2 = ((bf16[16,16,1024]{2,1,0:T(8,128)(2,1)}), bf16[16,16,1024]{2,1,0:T(8,128)(2,1)}, u32[]{:S(2)}, u32[]{:S(2)}) async-start(bf16[16,16,1024]{2,1,0:T(8,128)(2,1)} %convert_element_type.61), calls=%async_computation.2 | async-start | bytes 1048576 | tf_op jit(solution)/shard_map/all_to_all | solution.py:101
  117.3 14.4 %all-to-all-done.2 = bf16[16,16,1024]{2,1,0:T(8,128)(2,1)} async-done(((bf16[16,16,1024]{2,1,0:T(8,128)(2,1)}), bf16[16,16,1024]{2,1,0:T(8,128)(2,1)}, u32[]{:S(2)}, u32[]{:S(2)}) %all-to-all-start.2) | async-done | bytes 524320 | tf_op jit(solution)/shard_map/all_to_all | solution.py:101
  133.8 4.9 %convolution_bitcast_fusion = f32[1024,1024]{0,1:T(8,128)} fusion(bf16[128,1024]{1,0:T(8,128)(2,1)} %param.8, bf16[128,1024]{1,0:T(8,128)(2,1)S(1)} %gather_fusion.4, f32[128,1024]{1,0:T(8,128)} %get-tuple-element.59), kind=kOutput, calls=%fused_computation.12 | convolution fusion | flops 278003712 | bytes 5242880 | tf_op jit(solution)/shard_map/dot_general | solution.py:107
  138.8 5.3 %copy.115 = f32[1024,1024]{1,0:T(8,128)} copy(f32[1024,1024]{0,1:T(8,128)} %convolution_bitcast_fusion) | data formatting | bytes 8388608
  148.0 2.4 scatter_custom_fusion.6
  151.1 3.7 %all-to-all-start.4 = ((f32[16,1,256]{2,1,0:T(1,128)}), f32[16,1,256]{2,1,0:T(1,128)S(1)}, u32[]{:S(2)}, u32[]{:S(2)}) async-start(f32[16,1,256]{2,1,0:T(1,128)} %reshape.237), calls=%async_computation.4 | async-start | bytes 32768 | tf_op jit(solution)/shard_map/all_to_all | solution.py:117
  154.7 4.2 %fusion.23 = f32[256,8,128]{2,1,0:T(8,128)} fusion(f32[256,8,8]{2,1,0:T(8,128)} %copy.109, f32[256,8,128]{2,1,0:T(8,128)S(1)} %bitcast.100, f32[256,8]{1,0:T(8,128)S(1)} %copy.98), kind=kOutput, calls=%fused_computation.46 | convolution fusion | flops 25427968 | bytes 2170880 | tf_op jit(solution)/shard_map/transpose(jvp(npk,nqk->npq))/dot_general | solution.py:18
  159.0 2.9 %fusion.21 = f32[256,8,128]{2,1,0:T(8,128)} fusion(f32[256,8,8]{2,1,0:T(8,128)S(1)} %copy-done.2, f32[256,8,128]{2,1,0:T(8,128)S(1)} %bitcast.101, f32[256,8]{1,0:T(8,128)S(1)} %copy.98), kind=kOutput, calls=%fused_computation.44 | convolution fusion | flops 25427968 | bytes 2170880 | tf_op jit(solution)/shard_map/transpose(jvp(npk,nqk->npq))/dot_general | solution.py:18
  161.9 3.9 %scatter_custom_fusion.3 = f32[64,1024]{1,0:T(8,128)S(1)} fusion(s32[256]{0:T(256)} %bitcast.126, f32[32,8,8,128]{3,2,1,0:T(8,128)} %bitcast.107, f32[]{:T(128)} %constant.47.clone.1), kind=kCustom, calls=%fused_computation.36 | custom fusion | flops 262144 | bytes 1311232 | tf_op jit(solution)/shard_map/scatter-add | solution.py:37
  165.8 4.3 %scatter_custom_fusion.4 = f32[64,1024]{1,0:T(8,128)} fusion(s32[256]{0:T(256)S(1)} %bitcast.124, f32[32,8,8,128]{3,2,1,0:T(8,128)} %bitcast.106, f32[]{:T(128)} %constant.47.clone.1), kind=kCustom, calls=%fused_computation.33 | custom fusion | flops 262144 | bytes 1310724 | tf_op jit(solution)/shard_map/scatter-add | solution.py:37
  173.4 6.0 %all-to-all-start.3 = ((f32[16,4,1024]{2,1,0:T(4,128)}), f32[16,4,1024]{2,1,0:T(4,128)S(1)}, u32[]{:S(2)}, u32[]{:S(2)}) async-start(f32[16,4,1024]{2,1,0:T(4,128)} %all_to_all.33), calls=%async_computation.3 | async-start | bytes 524288 | tf_op jit(solution)/shard_map/all_to_all | solution.py:116
  179.5 39.3 %reduce-scatter.4.cloned.1.call-done = f32[64,1024]{1,0:T(8,128)} async-done(((f32[1024,1024]{1,0:T(8,128)}), f32[64,1024]{1,0:T(8,128)}) %reduce-scatter.4.cloned.1.call-update) | async-done | bytes 262160
  220.7 3.6 %scatter_custom_fusion.2 = f32[128,1024]{1,0:T(8,128)} fusion(s32[256]{0:T(256)S(1)} %bitcast.122, f32[32,8,8,128]{3,2,1,0:T(8,128)S(1)} %bitcast.108, f32[]{:T(128)} %constant.47.clone.1), kind=kCustom, calls=%fused_computation.39 | custom fusion | flops 262144 | bytes 1572868 | tf_op jit(solution)/shard_map/scatter-add | solution.py:37
  226.9 22.0 %all-reduce.4.cloned.1.call-done = f32[64,1024]{0,1:T(8,128)} async-done(((f32[64,1024]{0,1:T(8,128)}), f32[64,1024]{0,1:T(8,128)}) %all-reduce.4.cloned.1.call-update) | async-done | bytes 262160 | tf_op jit(solution)/shard_map/psum | solution.py:114
  (100 shorter events, 46.1 us)
Async XLA Ops:
  7.2 18.7 %copy-start = (bf16[1024,1024]{1,0:T(8,128)(2,1)S(1)}, bf16[1024,1024]{1,0:T(8,128)(2,1)}, u32[]{:S(2)}) copy-start(bf16[1024,1024]{1,0:T(8,128)(2,1)} %param.9) | copy-start | bytes 6291460
  7.2 8.5 %copy-start.1 = (s32[128]{0:T(128)S(1)}, s32[128]{0:T(128)}, u32[]{:S(2)}) copy-start(s32[128]{0:T(128)} %param.12) | copy-start | bytes 1540
  7.2 18.7 %copy-start.13 = (bf16[128,1024]{1,0:T(8,128)(2,1)S(1)}, bf16[128,1024]{1,0:T(8,128)(2,1)}, u32[]{:S(2)}) copy-start(bf16[128,1024]{1,0:T(8,128)(2,1)} %param.8) | copy-start | bytes 786436
  8.9 1.1 copy-start.11
  18.4 14.0 %all-to-all-start = ((s32[16,16,4]{1,2,0:T(4,128)}), s32[16,16,4]{1,2,0:T(4,128)S(1)}, u32[]{:S(2)}, u32[]{:S(2)}) async-start(s32[16,16,4]{1,2,0:T(4,128)} %copy.95), calls=%async_computation | async-start | bytes 65536 | tf_op jit(solution)/shard_map/all_to_all | solution.py:66
  29.2 7.0 %copy-start.9 = (bf16[4,1024]{1,0:T(4,128)(2,1)S(1)}, bf16[4,1024]{1,0:T(4,128)(2,1)}, u32[]{:S(2)}) copy-start(bf16[4,1024]{1,0:T(4,128)(2,1)} %param.14) | copy-start | bytes 24580
  29.2 32.3 %copy-start.10 = (bf16[4,64]{1,0:T(4,128)(2,1)S(1)}, bf16[4,64]{1,0:T(4,128)(2,1)}, u32[]{:S(2)}) copy-start(bf16[4,64]{1,0:T(4,128)(2,1)} %param.15) | copy-start | bytes 1540
  32.4 51.9 %all-to-all-start.1 = ((bf16[16,16,1024]{2,1,0:T(8,128)(2,1)}), bf16[16,16,1024]{2,1,0:T(8,128)(2,1)S(1)}, u32[]{:S(2)}, u32[]{:S(2)}) async-start(bf16[16,16,1024]{2,1,0:T(8,128)(2,1)} %broadcast_select_fusion), calls=%async_computation.1 | async-start | bytes 1048576 | tf_op jit(solution)/shard_map/all_to_all | solution.py:65
  82.7 1.6 copy-start.6
  100.5 3.9 %copy-start.3 = (f32[256,8,8]{2,1,0:T(8,128)S(1)}, f32[256,8,8]{2,1,0:T(8,128)}, u32[]{:S(2)}) copy-start(f32[256,8,8]{2,1,0:T(8,128)} %copy.109) | copy-start | bytes 196612
  100.5 3.9 %copy-start.4 = (f32[32,8,8,128]{3,2,1,0:T(8,128)S(1)}, f32[32,8,8,128]{3,2,1,0:T(8,128)}, u32[]{:S(2)}) copy-start(f32[32,8,8,128]{3,2,1,0:T(8,128)} %copy.120) | copy-start | bytes 3145732
  108.0 9.3 %copy-start.12 = (s32[128]{0:T(128)S(1)}, s32[128]{0:T(128)}, u32[]{:S(2)}) copy-start(s32[128]{0:T(128)} %copy-done.11) | copy-start | bytes 1540
  113.0 18.7 %all-to-all-start.2 = ((bf16[16,16,1024]{2,1,0:T(8,128)(2,1)}), bf16[16,16,1024]{2,1,0:T(8,128)(2,1)}, u32[]{:S(2)}, u32[]{:S(2)}) async-start(bf16[16,16,1024]{2,1,0:T(8,128)(2,1)} %convert_element_type.61), calls=%async_computation.2 | async-start | bytes 1048576 | tf_op jit(solution)/shard_map/all_to_all | solution.py:101
  117.2 101.5 %reduce-scatter.4.cloned.1.call-start = ((), (), s32[]{:S(2)}) async-start(), calls=%async_computation.7 | async-start | bytes 4456448
  144.1 0.8 copy-start.8
  144.1 0.9 copy-start.7
  151.1 22.4 %all-to-all-start.4 = ((f32[16,1,256]{2,1,0:T(1,128)}), f32[16,1,256]{2,1,0:T(1,128)S(1)}, u32[]{:S(2)}, u32[]{:S(2)}) async-start(f32[16,1,256]{2,1,0:T(1,128)} %reshape.237), calls=%async_computation.4 | async-start | bytes 32768 | tf_op jit(solution)/shard_map/all_to_all | solution.py:117
  154.7 4.2 %copy-start.2 = (f32[256,8,8]{2,1,0:T(8,128)S(1)}, f32[256,8,8]{2,1,0:T(8,128)}, u32[]{:S(2)}) copy-start(f32[256,8,8]{2,1,0:T(8,128)} %copy.110) | copy-start | bytes 196612
  165.7 55.0 %copy-start.5 = (f32[256,8,128]{2,1,0:T(8,128)S(1)}, f32[256,8,128]{2,1,0:T(8,128)}, u32[]{:S(2)}) copy-start(f32[256,8,128]{2,1,0:T(8,128)} %get-tuple-element.41) | copy-start | bytes 3145732
  173.4 52.8 %all-to-all-start.3 = ((f32[16,4,1024]{2,1,0:T(4,128)}), f32[16,4,1024]{2,1,0:T(4,128)S(1)}, u32[]{:S(2)}, u32[]{:S(2)}) async-start(f32[16,4,1024]{2,1,0:T(4,128)} %all_to_all.33), calls=%async_computation.3 | async-start | bytes 524288 | tf_op jit(solution)/shard_map/all_to_all | solution.py:116
  179.4 69.4 %all-reduce.4.cloned.1.call-start = ((), (), s32[]{:S(2)}) async-start(), calls=%async_computation.6 | async-start | bytes 1048576 | tf_op jit(solution)/shard_map/psum | solution.py:114
Sparse Core Ops, SparseCore 0:
  144.3 74.4 reduce-scatter.3
  221.1 27.6 all-reduce.3
where the time goes:
time: 259 us; the launch traced here: 258 us
  waiting for transfers between devices  78 us (30%)
  blocking collectives  44.4 us (17%)
  local copies, waits for them, and re-layouts  37.7 us (15%)
  matrix products  32 us (12%)
  other arithmetic  26.1 us (10%)
  starting transfers between devices  25 us (10%)
  between operations  14.4 us (6%)
    unnamed x3, waiting for transfers between devices  39.3 us
    all_gather x1, blocking collectives, local(): lax.all_gather(user_comps, 'shard', axis=0, tiled=True)  25.4 us
    dot_general x6, matrix products, mixture_score(): logits = jnp.einsum('npk,nqk->npq', users, normed, precision=highest)  22.5 us
    psum x1, waiting for transfers between devices, local(): tower_grad = lax.psum(partial_value, 'group')  22 us
    all_gather x1, blocking collectives, local(): lax.all_gather(user_gates, 'shard', axis=0, tiled=True)  19 us
    scatter-add x5, other arithmetic, spread_back(): jnp.zeros((row_total, values.shape[1]), jnp.float32).at[index].add(values)  16.2 us
    all_to_all x1, waiting for transfers between devices, local(): lax.all_to_all(derivs[0].astype(jnp.bfloat16), 'shard', split_axis=0, con...  14.4 us
    unnamed x37, local copies, waits for them, and re-layouts  13.5 us
  transfers between devices with their start and end apart: 7, of which 4 were waited for; matrix products, arithmetic and copies ran while one was open for 15% of the time, Pallas kernels for 0%

commit v1 on v0

v1 whole, which is shorter than its diff:
```python
import functools
import math

import jax
import jax.numpy as jnp
import numpy as np
from jax import lax
from jax.experimental import pallas as pl
from jax.experimental.pallas import tpu as pltpu
from jax.sharding import Mesh, PartitionSpec as P

COMPS = 8
KINDS = 4
LANES = 128
F32 = jnp.float32
BF16 = jnp.bfloat16
VMEM_LIMIT = 48 * 1024 * 1024


def iota(shape, axis):
    return lax.broadcasted_iota(jnp.int32, shape, axis)


def split_by(numbers, size):
    quotient = jnp.floor((numbers.astype(F32) + 0.5) * (1.0 / size)).astype(jnp.int32)
    return quotient, numbers - quotient * size


def nn(a, b):
    return lax.dot_general(a, b, (((1,), (0,)), ((), ())), preferred_element_type=F32)


def nt(a, b):
    return lax.dot_general(a, b, (((1,), (1,)), ((), ())), preferred_element_type=F32)


def halves(values):
    high = values.astype(BF16)
    return high, (values - high.astype(F32)).astype(BF16)


def erf(x):
    x = jnp.clip(x, -3.832506856900711, 3.832506856900711)
    s = x * x
    top = 0.00022905065861350646
    for c in (0.0034082910107109506, 0.050955695062380861, 0.18520832239976145, 1.128379143519084):
        top = top * s + c
    low = -1.1791602954361697e-7
    for c in (
        0.000023547966471313185,
        0.0010179625278914885,
        0.014070470171167667,
        0.11098505178285362,
        0.49746925110067538,
        1.0,
    ):
        low = low * s + c
    return x * top / low


def pack_kernel(cap, block, x_ref, owner_ref, slot_ref, pair_ref, user_ref, gate_ref, out_ref):
    items = x_ref.shape[0]
    rows = out_ref.shape[0]
    held = user_ref.shape[0]
    wide = (items, items)
    own_i = jnp.broadcast_to(owner_ref[...].astype(F32), wide)
    own_j = jnp.transpose(own_i)
    i, j = iota(wide, 0), iota(wide, 1)
    same = own_i == own_j
    rank_row = jnp.sum(jnp.where(same & (i < j), 1.0, 0.0), axis=0, keepdims=True)
    rank_col = jnp.sum(jnp.where(same & (j < i), 1.0, 0.0), axis=1, keepdims=True)
    slot_col = jnp.sum(
        jnp.where(i == j, jnp.broadcast_to(slot_ref[...].astype(F32), wide), 0.0), axis=1, keepdims=True
    )
    own_row = own_j[0:1, :]
    row_ids = iota((rows, items), 0)
    place = (own_row * block + rank_row).astype(jnp.int32)
    select = (row_ids == place).astype(F32).astype(BF16)
    _, spot = split_by(iota((rows, held), 0), block)
    lane = iota((rows, held), 1)
    main = nn(select, x_ref[...]) + nn(
        (spot == lane + cap).astype(F32).astype(BF16), user_ref[...]
    )
    width = gate_ref.shape[1]
    padded = nn(
        gate_ref[...], (iota((width, LANES), 0) == iota((width, LANES), 1)).astype(F32).astype(BF16)
    ).astype(BF16)
    gates = nn((spot == lane + cap + held).astype(F32).astype(BF16), padded)
    kind, turn = split_by(iota((items, LANES), 1), cap)
    pairs = pair_ref[...].astype(F32)
    value = jnp.where(
        kind == 0,
        slot_col,
        jnp.where(kind == 1, pairs[:, 0:1], jnp.where(kind == 2, pairs[:, 1:2], 1.0)),
    )
    value = jnp.where((kind < KINDS) & (rank_col.astype(jnp.int32) == turn), value, 0.0)
    to_owner = row_ids == (own_row * block + (cap + held)).astype(jnp.int32)
    header = nn(to_owner.astype(F32).astype(BF16), value.astype(BF16))
    out_ref[:, :LANES] = (main[:, :LANES] + gates).astype(BF16)
    out_ref[:, LANES : 2 * LANES] = (main[:, LANES : 2 * LANES] + header).astype(BF16)
    out_ref[:, 2 * LANES :] = main[:, 2 * LANES :].astype(BF16)


def train_kernel(
    shards, cap, block, held, order,
    recv_ref, wt_ref, table_t_ref,
    table_grad_ref, user_ref, xt_ref, dpt_ref,
    comp_ref, pos_ref, neg_ref, dpos_ref, dneg_ref, norm_ref, pre_ref, scale_ref,
):
    rows, width = recv_ref.shape
    slots = shards * cap
    users = shards * held
    comps = COMPS
    size = width // comps
    tables = table_t_ref.shape[1]
    recv = recv_ref[...]

    def rows_of(count, per, first):
        quotient, rest = split_by(iota((count, rows), 0), per)
        picked = iota((count, rows), 1) == quotient * block + first + rest
        return picked.astype(F32).astype(BF16)

    x_rows = nn(rows_of(slots, cap, 0), recv)
    x_t = jnp.transpose(x_rows).astype(BF16)
    unit = width // shards
    for place, first in enumerate(order):
        xt_ref[place * unit : (place + 1) * unit, :] = x_t[first * unit : (first + 1) * unit, :]
    user_rows = nn(rows_of(users, held, cap), recv)
    for p in range(comps):
        comp_ref[pl.ds(p, users, stride=comps), :] = user_rows[:, p * size : (p + 1) * size]
    comp_rows = comp_ref[...].astype(BF16)
    comp_t = jnp.transpose(comp_ref[...]).astype(BF16)
    gates_t = jnp.transpose(nn(rows_of(users, held, cap + held), recv[:, :LANES]))[: comps * comps]
    pairs = (comps * comps, comps * comps)
    outer, inner = split_by(iota(pairs, 0), comps)
    swap = (iota(pairs, 1) == inner * comps + outer).astype(F32).astype(BF16)
    gates_t = nn(swap, gates_t.astype(BF16)).astype(BF16)

    raw = nn(rows_of(shards, 1, cap + held), recv[:, LANES : 2 * LANES])
    source, turn = split_by(iota((shards, slots), 1), cap)
    spread = (source == iota((shards, slots), 0)).astype(F32).astype(BF16)
    fields = nn(jnp.transpose(raw).astype(BF16), spread)
    kind, field_turn = split_by(iota((LANES, slots), 0), cap)
    _, slot_turn = split_by(iota((LANES, slots), 1), cap)
    fields = jnp.where(field_turn == slot_turn, fields, 0.0)

    def field(number):
        return jnp.sum(jnp.where(kind == number, fields, 0.0), axis=0, keepdims=True)

    table_row = field(0).astype(jnp.int32)
    pos_row = field(1).astype(jnp.int32)
    neg_row = field(2).astype(jnp.int32)
    present = field(3)
    pick_table = (iota((tables, slots), 0) == table_row).astype(F32).astype(BF16)
    user_ids = iota((users, slots), 0)
    gate_pos = nn(gates_t, (user_ids == pos_row).astype(F32).astype(BF16))
    gate_neg = nn(gates_t, (user_ids == neg_row).astype(F32).astype(BF16))
    comp_twice = jnp.concatenate([comp_rows, comp_rows], axis=1)
    ids3 = iota((users, comps, slots), 0)
    is_pos = ids3 == pos_row[None]
    is_neg = ids3 == neg_row[None]

    for q in range(comps):
        part = slice(q * size, (q + 1) * size)
        pre = nn(wt_ref[part, :], x_t)
        pre_ref[part, :] = pre
        embedded = (0.5 * pre * (1.0 + erf(pre * math.sqrt(0.5)))).astype(BF16).astype(F32)
        combined = embedded + nn(table_t_ref[part, :], pick_table)
        scale = lax.rsqrt(jnp.mean(combined * combined, axis=0, keepdims=True) + 1e-06)
        scale_ref[q : q + 1, :] = scale
        normed = combined * scale
        norm_ref[part, :] = normed
        high, low = halves(normed)
        logits = nn(comp_twice, jnp.concatenate([high, low], axis=0))
        logits = logits.reshape(users, comps, slots)
        pos_ref[q * comps : (q + 1) * comps, :] = jnp.sum(jnp.where(is_pos, logits, 0.0), axis=0)
        neg_ref[q * comps : (q + 1) * comps, :] = jnp.sum(jnp.where(is_neg, logits, 0.0), axis=0)

    def side(logits, gates, sign):
        weights = jax.nn.sigmoid(gates + logits)
        score = 0.125 * jnp.sum(weights * logits, axis=0, keepdims=True)
        d_score = 0.125 * sign * jax.nn.sigmoid(sign * score) * present
        d_gates = d_score * (logits * weights * (1.0 - weights))
        return d_gates + d_score * weights, d_gates

    d_pos, dg_pos = side(pos_ref[...], gate_pos, -1.0)
    d_neg, dg_neg = side(neg_ref[...], gate_neg, 1.0)
    dpos_ref[...] = d_pos
    dneg_ref[...] = d_neg

    pad = -(-held // 8) * 8
    mate, rest = split_by(iota((shards * pad, slots), 0), pad)
    person = jnp.where(rest < held, mate * held + rest, -1)
    mask_pos = (person == pos_row).astype(F32).astype(BF16)
    mask_neg = (person == neg_row).astype(F32).astype(BF16)
    d_gate = jnp.zeros((shards * pad, comps * comps), F32)
    for mask, values in ((mask_pos, dg_pos), (mask_neg, dg_neg)):
        for piece in halves(values):
            d_gate = d_gate + nt(mask, nn(swap, piece).astype(BF16))
    own = held * comps
    user_ref[:, own:, : comps * comps] = d_gate.reshape(shards, pad, comps * comps)
    user_ref[:, own:, comps * comps :] = jnp.zeros(
        (shards, pad, size - comps * comps), F32
    )

    d_users = jnp.zeros((users * comps, size), F32)
    for q in range(comps):
        part = slice(q * size, (q + 1) * size)
        d_logit_pos = dpos_ref[q * comps : (q + 1) * comps, :][None]
        d_logit_neg = dneg_ref[q * comps : (q + 1) * comps, :][None]
        dense = jnp.where(is_pos, d_logit_pos, 0.0) + jnp.where(is_neg, d_logit_neg, 0.0)
        dense_high, dense_low = halves(dense.reshape(users * comps, slots))
        normed = norm_ref[part, :]
        high, low = halves(normed)
        d_users = d_users + nt(dense_high, high) + nt(dense_high, low) + nt(dense_low, high)
        d_normed = nn(comp_t, dense_high) + nn(comp_t, dense_low)
        inner = jnp.mean(d_normed * normed, axis=0, keepdims=True)
        d_combined = scale_ref[q : q + 1, :] * (d_normed - normed * inner)
        total = jnp.zeros((tables, size), F32)
        for piece in halves(d_combined):
            total = total + nt(pick_table, piece)
        table_grad_ref[:, part] = total
        pre = pre_ref[part, :]
        slope = 0.5 * (1.0 + erf(pre * math.sqrt(0.5))) + pre * (
            jnp.exp(-0.5 * pre * pre) * (1.0 / math.sqrt(2.0 * math.pi))
        )
        dpt_ref[part, :] = (d_combined.astype(BF16).astype(F32) * slope).astype(BF16)
    user_ref[:, :own, :] = d_users.reshape(shards, own, size)


def tower_kernel(groups, x_ref, x_far_ref, d_ref, d_far_ref, out_ref):
    wide = d_ref.shape[0] // groups
    for g in range(groups):
        part = slice(g * wide, (g + 1) * wide)
        out_ref[g] = (
            nt(x_ref[...], d_ref[part, :]) + nt(x_far_ref[...], d_far_ref[part, :])
        ).astype(BF16)


def local(
    sizes, item_features, tower_weight, item_table, owner, table_slot, pair_users, user_comps, user_gates
):
    groups, deep, across, cores = sizes
    shards = deep * across * cores
    shard_axes = ("z", "x", "core")
    items, width = item_features.shape
    cap = max(1, 2 * items // shards)
    held = user_comps.shape[0]
    block = -(-(cap + 2 * held) // 8) * 8
    rows = shards * block
    slots = shards * cap
    size = width // COMPS
    users = shards * held
    params = pltpu.CompilerParams(vmem_limit_bytes=VMEM_LIMIT)

    packed = pl.pallas_call(
        functools.partial(pack_kernel, cap, block),
        out_shape=jax.ShapeDtypeStruct((rows, width), BF16),
        compiler_params=params,
        name="pack",
    )(item_features, owner, table_slot.reshape(1, items), pair_users, user_comps, user_gates)
    recv = lax.all_to_all(packed, shard_axes, split_axis=0, concat_axis=0, tiled=True)
    weight_t = tower_weight.T
    table_t = item_table.T

    order = [
        (z * across + x) * cores + c for c in range(cores) for x in range(across) for z in range(deep)
    ]
    own = held * COMPS
    pad = -(-held // 8) * 8
    table_grad, user_part, x_t, dp_t = pl.pallas_call(
        functools.partial(train_kernel, shards, cap, block, held, order),
        out_shape=(
            jax.ShapeDtypeStruct((item_table.shape[0], width), F32),
            jax.ShapeDtypeStruct((shards, own + pad, size), F32),
            jax.ShapeDtypeStruct((width, slots), BF16),
            jax.ShapeDtypeStruct((width, slots), BF16),
        ),
        scratch_shapes=[
            pltpu.VMEM((users * COMPS, size), F32),
            pltpu.VMEM((COMPS * COMPS, slots), F32),
            pltpu.VMEM((COMPS * COMPS, slots), F32),
            pltpu.VMEM((COMPS * COMPS, slots), F32),
            pltpu.VMEM((COMPS * COMPS, slots), F32),
            pltpu.VMEM((width, slots), F32),
            pltpu.VMEM((width, slots), F32),
            pltpu.VMEM((COMPS, slots), F32),
        ],
        compiler_params=params,
        name="train",
    )(recv, weight_t, table_t)

    core = lax.axis_index("core")
    half = width // cores
    swap = [(0, 1), (1, 0)]
    x_own = lax.dynamic_slice_in_dim(x_t, core * half, half, 0)
    x_far = lax.ppermute(lax.dynamic_slice_in_dim(x_t, (1 - core) * half, half, 0), "core", swap)
    dp_far = lax.ppermute(dp_t, "core", swap)
    part = pl.pallas_call(
        functools.partial(tower_kernel, groups),
        out_shape=jax.ShapeDtypeStruct((groups, half, width // groups), BF16),
        compiler_params=params,
        name="tower",
    )(x_own, x_far, dp_t, dp_far)
    wide = width // groups
    got = lax.all_to_all(
        part.reshape(groups * across, half // across, wide), ("y", "x"), split_axis=0, concat_axis=0, tiled=True
    )
    summed = jnp.sum(got.astype(F32), axis=0).astype(BF16)
    got = lax.all_to_all(
        summed.reshape(deep, half // across // deep, wide), "z", split_axis=0, concat_axis=0, tiled=True
    )
    mine = jnp.sum(got.astype(F32), axis=0)
    if groups == 2:
        other = lax.ppermute(mine, "y", swap)
        first = lax.axis_index("y") == 0
        tower_grad = jnp.concatenate(
            [jnp.where(first, mine, other), jnp.where(first, other, mine)], axis=1
        )
    else:
        tower_grad = lax.all_gather(mine, "y", axis=1, tiled=True)

    got_users = lax.all_to_all(user_part, shard_axes, split_axis=0, concat_axis=0, tiled=True)
    user_sum = jnp.sum(got_users, axis=0)
    user_comp_grad = user_sum[:own].reshape(held, width)
    user_gate_grad = user_sum[own : own + held, : COMPS * COMPS]
    return tower_grad, table_grad, user_comp_grad, user_gate_grad


def solution(mesh):
    groups, shards = mesh.shape["group"], mesh.shape["shard"]
    cores = 2
    chips = shards // cores
    across = 1
    while 8 * across * across <= chips:
        across *= 2
    sizes = (groups, chips // across, across, cores)
    fine = Mesh(np.asarray(mesh.devices).reshape(sizes), ("y", "z", "x", "core"))
    whole = ("y", "z", "x", "core")
    placed = (
        P(whole, None), P(), P(whole, None), P(whole, None),
        P(whole), P(whole, None), P(whole, None), P(whole, None),
    )
    return jax.shard_map(
        functools.partial(local, sizes),
        mesh=fine,
        in_specs=placed,
        out_specs=(
            P(("z", "x", "core"), None), P(whole, None), P(whole, None), P(whole, None),
        ),
        check_vma=False,
    )
```

time: 259 us -> 95.9 us (0.37)
  waiting for transfers between devices: 78 us -> 26.6 us
  matrix products: 32 us -> 0 us
  local copies, waits for them, and re-layouts: 37.7 us -> 10.7 us
  other arithmetic: 26.1 us -> 1.04 us
  blocking collectives: 44.4 us -> 30.1 us
  between operations: 14.4 us -> 0.73 us
  Pallas kernels: 0 us -> 13.3 us
  starting transfers between devices: 25 us -> 12.7 us
    all_gather x2 -> x0, blocking collectives: 44.4 us -> none  [the longest x1 25.4 us: local(): lax.all_gather(user_comps, 'shard', axis=0, tiled=True)]
    unnamed x3 -> x0, waiting for transfers between devices: 39.3 us -> none
    dot_general x14 -> x0, matrix products: 32 us -> none  [the longest x6 22.5 us: mixture_score(): logits = jnp.einsum('npk,nqk->npq', users, normed, precision=highest)]
    all_to_all x0 -> x2, blocking collectives: none -> 30.1 us  [the longest x1 18.1 us: local(): lax.all_to_all(part.reshape(groups * across, half // across, wide), ('y',...]
    psum x1 -> x0, waiting for transfers between devices: 22 us -> none  [local(): tower_grad = lax.psum(partial_value, 'group')]
    scatter-add x5 -> x0, other arithmetic: 16.2 us -> none  [spread_back(): jnp.zeros((row_total, values.shape[1]), jnp.float32).at[index].add(values)]
    all_to_all x5 -> x2, starting transfers between devices: 25 us -> 10.9 us  [the longest x1 7.36 us: local(): lax.all_to_all(packed, shard_axes, split_axis=0, concat_axis=0, tiled=True)]
    pallas_call x0 -> x3, Pallas kernels: none -> 13.3 us  [the longest x1 9.95 us: local(): pl.pallas_call(functools.partial(train_kernel, shards, cap, block, held,...]
  transfers between devices with their start and end apart: 7 -> 5, of which waited for: 4 -> 3; matrix products, arithmetic and copies ran while one was open for 15% -> 6% of each run, Pallas kernels for 0% -> 0%
where the time goes in v1:
time: 95.9 us; the launch traced here: 95.3 us
  blocking collectives  30.1 us (31%)
  waiting for transfers between devices  26.6 us (28%)
  Pallas kernels  13.3 us (14%)
  starting transfers between devices  12.7 us (13%)
  local copies, waits for them, and re-layouts  10.7 us (11%)
  other arithmetic  1.04 us (1%)
    all_to_all x1, blocking collectives, local(): lax.all_to_all(part.reshape(groups * across, half // across, wide), ('y',...  18.1 us
    all_to_all x1, waiting for transfers between devices, local(): lax.all_to_all(packed, shard_axes, split_axis=0, concat_axis=0, tiled=True)  15.6 us
    all_to_all x1, blocking collectives, local(): lax.all_to_all(summed.reshape(deep, half // across // deep, wide), 'z', s...  12.1 us
    pallas_call x1, Pallas kernels, local(): pl.pallas_call(functools.partial(train_kernel, shards, cap, block, held,...  9.95 us
    all_to_all x1, waiting for transfers between devices, local(): lax.all_to_all(user_part, shard_axes, split_axis=0, concat_axis=0, tiled=...  9.75 us
    unnamed x16, local copies, waits for them, and re-layouts  8.39 us
    all_to_all x1, starting transfers between devices, local(): lax.all_to_all(packed, shard_axes, split_axis=0, concat_axis=0, tiled=True)  7.36 us
    all_to_all x1, starting transfers between devices, local(): lax.all_to_all(user_part, shard_axes, split_axis=0, concat_axis=0, tiled=...  3.54 us
  transfers between devices with their start and end apart: 5, of which 3 were waited for; matrix products, arithmetic and copies ran while one was open for 6% of the time, Pallas kernels for 0%

profile of v1, /device:TPU:0, one launch (start us, length us, event | category | flops | bytes accessed | tf_op | source)
XLA Modules:
  0.0 95.3 jit_solution(5923299186293692896)
XLA Ops:
  0.6 0.8 copy.16.owner_ref
  1.4 0.8 copy.17.pair_ref
  2.2 0.9 copy-done.1
  3.1 0.7 copy-done.2
  3.8 0.7 copy-done.3
  4.5 0.7 copy-done.4
  5.2 1.6 %pack.1 = bf16[384,1024]{1,0:T(8,128)(2,1)} custom-call(bf16[128,1024]{1,0:T(8,128)(2,1)S(1)} %copy-done.1, s32[128,1]{1,0:T(8,128)S(1)} %copy.16.owner_ref, s32[1,128]{1,0:T(1,128)S(1)} %bitcast.11, s32[128,2]{1,0:T(8,128)S(1)} %copy.17.pair_ref, bf16[4,1024]{1,0:T(4,128)(2,1)S(1)} %copy-done.2, bf16[4,64]{1,0:T(4,128)(2,1)S(1)} %copy-done.3), custom_call_target="tpu_custom_call" | custom-call | tf_op jit(solution)/shard_map/pack/pallas_call | solution.py:256
  6.8 7.4 %all-to-all-start = ((bf16[16,24,1024]{2,1,0:T(8,128)(2,1)}), bf16[16,24,1024]{2,1,0:T(8,128)(2,1)S(1)}, u32[]{:S(2)}, u32[]{:S(2)}) async-start(bf16[16,24,1024]{2,1,0:T(8,128)(2,1)} %bitcast.1), calls=%async_computation | async-start | bytes 1572864 | tf_op jit(solution)/shard_map/all_to_all | solution.py:262
  14.2 2.9 %copy.18 = bf16[1024,1024]{0,1:T(8,128)(2,1)S(1)} copy(bf16[1024,1024]{1,0:T(8,128)(2,1)} %param.9) | data formatting | bytes 4194304 | tf_op args[1]
  17.3 15.6 %all-to-all-done = bf16[16,24,1024]{2,1,0:T(8,128)(2,1)S(1)} async-done(((bf16[16,24,1024]{2,1,0:T(8,128)(2,1)}), bf16[16,24,1024]{2,1,0:T(8,128)(2,1)S(1)}, u32[]{:S(2)}, u32[]{:S(2)}) %all-to-all-start) | async-done | bytes 786464 | tf_op jit(solution)/shard_map/all_to_all | solution.py:262
  32.9 9.9 %train.1 = (f32[128,1024]{1,0:T(8,128)}, f32[16,40,128]{2,1,0:T(8,128)}, bf16[1024,256]{1,0:T(8,128)(2,1)S(1)}, bf16[1024,256]{1,0:T(8,128)(2,1)}) custom-call(bf16[384,1024]{1,0:T(8,128)(2,1)S(1)} %bitcast.9, bf16[1024,1024]{1,0:T(8,128)(2,1)S(1)} %bitcast.7, bf16[1024,128]{1,0:T(8,128)(2,1)S(1)} %bitcast.10), custom_call_target="tpu_custom_call" | custom-call | tf_op jit(solution)/shard_map/train/pallas_call | solution.py:271
  42.8 0.8 copy-done
  43.8 1.1 %constant_dynamic-slice_fusion = (bf16[512,256]{1,0:T(8,128)(2,1)S(1)}, bf16[512,256]{1,0:T(8,128)(2,1)S(1)}) fusion(bf16[1024,256]{1,0:T(8,128)(2,1)} %copy-done, s32[]{:T(128)S(6)} %select_n.20, s32[]{:T(128)S(6)} %select_n.19), kind=kLoop, calls=%fused_computation.4 | loop fusion | bytes 1048584 | tf_op jit(solution)/shard_map/dynamic_slice | solution.py:297
  44.9 0.3 collective-permute-start
  45.2 1.3 %collective-permute-done.x_far_ref = bf16[512,256]{1,0:T(8,128)(2,1)S(1)} collective-permute-done((bf16[512,256]{1,0:T(8,128)(2,1)S(1)}, bf16[512,256]{1,0:T(8,128)(2,1)S(1)}, u32[]{:S(2)}, u32[]{:S(2)}) %collective-permute-start) | collective-permute-done | bytes 262176 | tf_op jit(solution)/shard_map/ppermute | solution.py:297
  46.5 1.8 %tower.1 = bf16[2,512,512]{2,1,0:T(8,128)(2,1)S(1)} custom-call(bf16[512,256]{1,0:T(8,128)(2,1)S(1)} %get-tuple-element.13.x_ref, bf16[512,256]{1,0:T(8,128)(2,1)S(1)} %collective-permute-done.x_far_ref, bf16[1024,256]{1,0:T(8,128)(2,1)} %get-tuple-element.9.d_ref, bf16[1024,256]{1,0:T(8,128)(2,1)S(1)} %collective-permute-done.1.d_far_ref), custom_call_target="tpu_custom_call" | custom-call | tf_op jit(solution)/shard_map/tower/pallas_call | solution.py:299
  48.3 18.1 %all_to_all.26 = bf16[4,256,512]{2,1,0:T(8,128)(2,1)S(1)} all-to-all(bf16[4,256,512]{2,1,0:T(8,128)(2,1)S(1)} %bitcast.8), channel_id=1, replica_groups=mesh['y'=2,'z'=4,'x'=2,'core'=2] {'y','x'}, dimensions={0} | all-to-all | bytes 2097152 | tf_op jit(solution)/shard_map/all_to_all | solution.py:306
  66.6 12.1 %all_to_all.27 = bf16[4,64,512]{2,1,0:T(8,128)(2,1)S(1)} all-to-all(bf16[4,64,512]{2,1,0:T(8,128)(2,1)S(1)} %bitcast.12), channel_id=1, replica_groups=mesh['y'=2,'z'=4,'x'=2,'core'=2] {'z'}, dimensions={0} | all-to-all | bytes 524288 | tf_op jit(solution)/shard_map/all_to_all | solution.py:310
  78.7 3.5 %all-to-all-start.3 = ((f32[16,40,128]{2,1,0:T(8,128)}), f32[16,40,128]{2,1,0:T(8,128)S(1)}, u32[]{:S(2)}, u32[]{:S(2)}) async-start(f32[16,40,128]{2,1,0:T(8,128)} %get-tuple-element.11), calls=%async_computation.3 | async-start | bytes 655360 | tf_op jit(solution)/shard_map/all_to_all | solution.py:323
  82.3 1.3 %collective-permute-start.2 = (f32[64,512]{1,0:T(8,128)S(1)}, f32[64,512]{1,0:T(8,128)S(1)}, u32[]{:S(2)}, u32[]{:S(2)}) collective-permute-start(f32[64,512]{1,0:T(8,128)S(1)} %convert_reduce_fusion), channel_id=1, source_target_pairs={{0,16},{16,0},{1,17},{17,1},{2,18},{18,2},{3,19},{19,3},{4,20},{20... | collective-permute-start | bytes 393224 | tf_op jit(solution)/shard_map/ppermute | solution.py:315
  83.6 9.8 %all-to-all-done.3 = f32[16,40,128]{2,1,0:T(8,128)S(1)} async-done(((f32[16,40,128]{2,1,0:T(8,128)}), f32[16,40,128]{2,1,0:T(8,128)S(1)}, u32[]{:S(2)}, u32[]{:S(2)}) %all-to-all-start.3) | async-done | bytes 327712 | tf_op jit(solution)/shard_map/all_to_all | solution.py:323
  93.3 0.6 slice.9
  93.9 0.6 reshape.25
  94.6 0.7 pad_maximum_fusion
  (16 shorter events, 0.8 us)
Async XLA Ops:
  2.2 0.9 copy-start.1
  3.1 0.7 copy-start.2
  3.8 0.7 copy-start.3
  4.5 0.7 copy-start.4
  6.8 26.1 %all-to-all-start = ((bf16[16,24,1024]{2,1,0:T(8,128)(2,1)}), bf16[16,24,1024]{2,1,0:T(8,128)(2,1)S(1)}, u32[]{:S(2)}, u32[]{:S(2)}) async-start(bf16[16,24,1024]{2,1,0:T(8,128)(2,1)} %bitcast.1), calls=%async_computation | async-start | bytes 1572864 | tf_op jit(solution)/shard_map/all_to_all | solution.py:262
  14.1 2.9 %copy-start.5 = (bf16[128,1024]{1,0:T(8,128)(2,1)S(1)}, bf16[128,1024]{1,0:T(8,128)(2,1)}, u32[]{:S(2)}) copy-start(bf16[128,1024]{1,0:T(8,128)(2,1)} %param.10) | copy-start | bytes 786436
  42.8 0.8 copy-start
  43.6 2.9 %collective-permute-start.1 = (bf16[1024,256]{1,0:T(8,128)(2,1)}, bf16[1024,256]{1,0:T(8,128)(2,1)S(1)}, u32[]{:S(2)}, u32[]{:S(2)}) collective-permute-start(bf16[1024,256]{1,0:T(8,128)(2,1)} %get-tuple-element.9.d_ref), channel_id=1, source_target_pairs={{0,1},{1,0},{2,3},{3,2},{4,5},{5,4},{6,7},{7,6},{8,9},{9,8},{10,11... | collective-permute-start | bytes 1572872 | tf_op jit(solution)/shard_map/ppermute | solution.py:298
  44.9 1.6 %collective-permute-start = (bf16[512,256]{1,0:T(8,128)(2,1)S(1)}, bf16[512,256]{1,0:T(8,128)(2,1)S(1)}, u32[]{:S(2)}, u32[]{:S(2)}) collective-permute-start(bf16[512,256]{1,0:T(8,128)(2,1)S(1)} %get-tuple-element.12), channel_id=1, source_target_pairs={{0,1},{1,0},{2,3},{3,2},{4,5},{5,4},{6,7},{7,6},{8,9},{9,8},{10,11... | collective-permute-start | bytes 786440 | tf_op jit(solution)/shard_map/ppermute | solution.py:297
  78.7 14.6 %all-to-all-start.3 = ((f32[16,40,128]{2,1,0:T(8,128)}), f32[16,40,128]{2,1,0:T(8,128)S(1)}, u32[]{:S(2)}, u32[]{:S(2)}) async-start(f32[16,40,128]{2,1,0:T(8,128)} %get-tuple-element.11), calls=%async_computation.3 | async-start | bytes 655360 | tf_op jit(solution)/shard_map/all_to_all | solution.py:323
  82.3 12.3 %collective-permute-start.2 = (f32[64,512]{1,0:T(8,128)S(1)}, f32[64,512]{1,0:T(8,128)S(1)}, u32[]{:S(2)}, u32[]{:S(2)}) collective-permute-start(f32[64,512]{1,0:T(8,128)S(1)} %convert_reduce_fusion), channel_id=1, source_target_pairs={{0,16},{16,0},{1,17},{17,1},{2,18},{18,2},{3,19},{19,3},{4,20},{20... | collective-permute-start | bytes 393224 | tf_op jit(solution)/shard_map/ppermute | solution.py:315

commit v2 on v1

--- a/solution.py
+++ b/solution.py
@@ -15,6 +15,8 @@
 F32 = jnp.float32
 BF16 = jnp.bfloat16
 VMEM_LIMIT = 48 * 1024 * 1024
+PACK_LIMIT = 60 * 1024 * 1024
+FEW = 4
 
 
 def iota(shape, axis):
@@ -63,15 +65,18 @@
     rows = out_ref.shape[0]
     held = user_ref.shape[0]
     wide = (items, items)
-    own_i = jnp.broadcast_to(owner_ref[...].astype(F32), wide)
-    own_j = jnp.transpose(own_i)
+    own_j = jnp.broadcast_to(owner_ref[...].astype(F32), wide)
+    own_i = jnp.transpose(own_j)
     i, j = iota(wide, 0), iota(wide, 1)
     same = own_i == own_j
     rank_row = jnp.sum(jnp.where(same & (i < j), 1.0, 0.0), axis=0, keepdims=True)
     rank_col = jnp.sum(jnp.where(same & (j < i), 1.0, 0.0), axis=1, keepdims=True)
-    slot_col = jnp.sum(
-        jnp.where(i == j, jnp.broadcast_to(slot_ref[...].astype(F32), wide), 0.0), axis=1, keepdims=True
-    )
+
+    def column(row):
+        return jnp.sum(jnp.where(i == j, row.astype(F32), 0.0), axis=1, keepdims=True)
+
+    slot_col = column(slot_ref[...])
+    first_col, second_col = column(pair_ref[0:1, :]), column(pair_ref[1:2, :])
     own_row = own_j[0:1, :]
     row_ids = iota((rows, items), 0)
     place = (own_row * block + rank_row).astype(jnp.int32)
@@ -87,11 +92,10 @@
     ).astype(BF16)
     gates = nn((spot == lane + cap + held).astype(F32).astype(BF16), padded)
     kind, turn = split_by(iota((items, LANES), 1), cap)
-    pairs = pair_ref[...].astype(F32)
     value = jnp.where(
         kind == 0,
         slot_col,
-        jnp.where(kind == 1, pairs[:, 0:1], jnp.where(kind == 2, pairs[:, 1:2], 1.0)),
+        jnp.where(kind == 1, first_col, jnp.where(kind == 2, second_col, 1.0)),
     )
     value = jnp.where((kind < KINDS) & (rank_col.astype(jnp.int32) == turn), value, 0.0)
     to_owner = row_ids == (own_row * block + (cap + held)).astype(jnp.int32)
@@ -103,8 +107,8 @@
 
 def train_kernel(
     shards, cap, block, held, order,
-    recv_ref, wt_ref, table_t_ref,
-    table_grad_ref, user_ref, xt_ref, dpt_ref,
+    core_ref, recv_ref, wt_ref, table_t_ref,
+    table_grad_ref, user_ref, x_own_ref, x_far_ref, dpt_ref,
     comp_ref, pos_ref, neg_ref, dpos_ref, dneg_ref, norm_ref, pre_ref, scale_ref,
 ):
     rows, width = recv_ref.shape
@@ -123,8 +127,13 @@
     x_rows = nn(rows_of(slots, cap, 0), recv)
     x_t = jnp.transpose(x_rows).astype(BF16)
     unit = width // shards
-    for place, first in enumerate(order):
-        xt_ref[place * unit : (place + 1) * unit, :] = x_t[first * unit : (first + 1) * unit, :]
+    first_core = core_ref[0] == 0
+    for place, (here, there) in enumerate(order):
+        into = slice(place * unit, (place + 1) * unit)
+        one = x_t[here * unit : (here + 1) * unit, :]
+        two = x_t[there * unit : (there + 1) * unit, :]
+        x_own_ref[into, :] = jnp.where(first_core, one, two)
+        x_far_ref[into, :] = jnp.where(first_core, two, one)
     user_rows = nn(rows_of(users, held, cap), recv)
     for p in range(comps):
         comp_ref[pl.ds(p, users, stride=comps), :] = user_rows[:, p * size : (p + 1) * size]
@@ -228,13 +237,50 @@
     user_ref[:, :own, :] = d_users.reshape(shards, own, size)
 
 
-def tower_kernel(groups, x_ref, x_far_ref, d_ref, d_far_ref, out_ref):
+def views(refs, count):
+    return list(refs) if len(refs) == count else [refs[0].at[k] for k in range(count)]
+
+
+def blocks(count, shape):
+    if count <= FEW:
+        return [jax.ShapeDtypeStruct(shape, BF16)] * count
+    return [jax.ShapeDtypeStruct((count,) + shape, BF16)]
+
+
+def partner_of(me_ref, k, count):
+    return me_ref[0] ^ k if count <= FEW else k
+
+
+def exchange(parts, axis, count):
+    if count > FEW:
+        return [lax.all_to_all(parts[0], axis, split_axis=0, concat_axis=0, tiled=True)]
+    return [parts[0]] + [
+        lax.ppermute(parts[k], axis, [(i, i ^ k) for i in range(count)]) for k in range(1, count)
+    ]
+
+
+def tower_kernel(groups, across, me_ref, x_ref, x_far_ref, d_ref, d_far_ref, *outs):
     wide = d_ref.shape[0] // groups
-    for g in range(groups):
-        part = slice(g * wide, (g + 1) * wide)
-        out_ref[g] = (
-            nt(x_ref[...], d_ref[part, :]) + nt(x_far_ref[...], d_far_ref[part, :])
+    tall = x_ref.shape[0] // across
+    count = groups * across
+    for k, out_ref in enumerate(views(outs, count)):
+        partner = partner_of(me_ref, k, count)
+        tower_rows = pl.ds(pl.multiple_of(lax.rem(partner, across) * tall, tall), tall)
+        columns = pl.ds(pl.multiple_of(lax.div(partner, across) * wide, wide), wide)
+        out_ref[...] = (
+            nt(x_ref[tower_rows, :], d_ref[columns, :]) + nt(x_far_ref[tower_rows, :], d_far_ref[columns, :])
         ).astype(BF16)
+
+
+def sum_kernel(given, count, deep, me_ref, *refs):
+    ins, outs = views(refs[:given], count), views(refs[given:], deep)
+    tall = outs[0].shape[0]
+    for k, out_ref in enumerate(outs):
+        part = pl.ds(pl.multiple_of(partner_of(me_ref, k, deep) * tall, tall), tall)
+        total = ins[0][part, :].astype(F32)
+        for in_ref in ins[1:]:
+            total = total + in_ref[part, :].astype(F32)
+        out_ref[...] = total.astype(BF16)
 
 
 def local(
@@ -256,26 +302,32 @@
     packed = pl.pallas_call(
         functools.partial(pack_kernel, cap, block),
         out_shape=jax.ShapeDtypeStruct((rows, width), BF16),
-        compiler_params=params,
+        compiler_params=pltpu.CompilerParams(vmem_limit_bytes=PACK_LIMIT),
         name="pack",
-    )(item_features, owner, table_slot.reshape(1, items), pair_users, user_comps, user_gates)
+    )(item_features, owner.T, table_slot.reshape(1, items), pair_users.T, user_comps, user_gates)
     recv = lax.all_to_all(packed, shard_axes, split_axis=0, concat_axis=0, tiled=True)
     weight_t = tower_weight.T
     table_t = item_table.T
 
     order = [
-        (z * across + x) * cores + c for c in range(cores) for x in range(across) for z in range(deep)
+        ((z * across + x) * cores, (z * across + x) * cores + 1) for x in range(across) for z in range(deep)
     ]
+    half = width // cores
+    core = lax.axis_index("core")
+    scalar = pl.BlockSpec(memory_space=pltpu.SMEM)
+    vmem = pl.BlockSpec(memory_space=pltpu.VMEM)
     own = held * COMPS
     pad = -(-held // 8) * 8
-    table_grad, user_part, x_t, dp_t = pl.pallas_call(
+    table_grad, user_part, x_own, x_send, dp_t = pl.pallas_call(
         functools.partial(train_kernel, shards, cap, block, held, order),
         out_shape=(
             jax.ShapeDtypeStruct((item_table.shape[0], width), F32),
             jax.ShapeDtypeStruct((shards, own + pad, size), F32),
-            jax.ShapeDtypeStruct((width, slots), BF16),
+            jax.ShapeDtypeStruct((half, slots), BF16),
+            jax.ShapeDtypeStruct((half, slots), BF16),
             jax.ShapeDtypeStruct((width, slots), BF16),
         ),
+        in_specs=[scalar, vmem, vmem, vmem],
         scratch_shapes=[
             pltpu.VMEM((users * COMPS, size), F32),
             pltpu.VMEM((COMPS * COMPS, slots), F32),
@@ -288,29 +340,33 @@
         ],
         compiler_params=params,
         name="train",
-    )(recv, weight_t, table_t)
-
-    core = lax.axis_index("core")
-    half = width // cores
+    )(core.reshape(1), recv, weight_t, table_t)
+
     swap = [(0, 1), (1, 0)]
-    x_own = lax.dynamic_slice_in_dim(x_t, core * half, half, 0)
-    x_far = lax.ppermute(lax.dynamic_slice_in_dim(x_t, (1 - core) * half, half, 0), "core", swap)
+    x_far = lax.ppermute(x_send, "core", swap)
     dp_far = lax.ppermute(dp_t, "core", swap)
-    part = pl.pallas_call(
-        functools.partial(tower_kernel, groups),
-        out_shape=jax.ShapeDtypeStruct((groups, half, width // groups), BF16),
+    partners = groups * across
+    tall, wide = half // across, width // groups
+    parts = pl.pallas_call(
+        functools.partial(tower_kernel, groups, across),
+        out_shape=blocks(partners, (tall, wide)),
+        in_specs=[scalar] + [vmem] * 4,
         compiler_params=params,
         name="tower",
-    )(x_own, x_far, dp_t, dp_far)
-    wide = width // groups
-    got = lax.all_to_all(
-        part.reshape(groups * across, half // across, wide), ("y", "x"), split_axis=0, concat_axis=0, tiled=True
-    )
-    summed = jnp.sum(got.astype(F32), axis=0).astype(BF16)
-    got = lax.all_to_all(
-        summed.reshape(deep, half // across // deep, wide), "z", split_axis=0, concat_axis=0, tiled=True
-    )
-    mine = jnp.sum(got.astype(F32), axis=0)
+    )(lax.axis_index(("y", "x")).reshape(1), x_own, x_far, dp_t, dp_far)
+    got = exchange(parts, ("y", "x"), partners)
+    parts = pl.pallas_call(
+        functools.partial(sum_kernel, len(got), partners, deep),
+        out_shape=blocks(deep, (tall // deep, wide)),
+        in_specs=[scalar] + [vmem] * len(got),
+        compiler_params=params,
+        name="sums",
+    )(lax.axis_index("z").reshape(1), *got)
+    got = exchange(parts, "z", deep)
+    if deep > FEW:
+        mine = jnp.sum(got[0].astype(F32), axis=0)
+    else:
+        mine = sum(part.astype(F32) for part in got)
     if groups == 2:
         other = lax.ppermute(mine, "y", swap)
         first = lax.axis_index("y") == 0

time: 95.9 us -> 77.5 us (0.81)
  blocking collectives: 30.1 us -> 0 us
  starting transfers between devices: 12.7 us -> 23.5 us
  waiting for transfers between devices: 26.6 us -> 33.3 us
  local copies, waits for them, and re-layouts: 10.7 us -> 4.28 us
  Pallas kernels: 13.3 us -> 14.4 us
    all_to_all x2 -> x0, blocking collectives: 30.1 us -> none  [the longest x1 18.1 us: local(): lax.all_to_all(part.reshape(groups * across, half // across, wide), ('y',...]
    ppermute x1 -> x7, waiting for transfers between devices: 1.28 us -> 14.6 us  [the longest x6 12.6 us: exchange(): lax.ppermute(parts[k], axis, [(i, i ^ k) for i in range(count)])]
    all_to_all x1, waiting for transfers between devices: 9.75 us -> 0.01 us  [local(): lax.all_to_all(user_part, shard_axes, split_axis=0, concat_axis=0, tiled=...]
    ppermute x1 -> x7, starting transfers between devices: 0.32 us -> 9.8 us  [the longest x6 9.54 us: exchange(): lax.ppermute(parts[k], axis, [(i, i ^ k) for i in range(count)])]
    unnamed x16 -> x4, local copies, waits for them, and re-layouts: 8.39 us -> 3.08 us
    ppermute x1, waiting for transfers between devices: 0.01 us -> 3.18 us  [local(): other = lax.ppermute(mine, 'y', swap)]
    all_to_all x1, starting transfers between devices: 3.54 us -> 5.49 us  [local(): lax.all_to_all(user_part, shard_axes, split_axis=0, concat_axis=0, tiled=...]
    dynamic_slice x1 -> x0, local copies, waits for them, and re-layouts: 1.06 us -> none  [local(): lax.dynamic_slice_in_dim(x_t, (1 - core) * half, half, 0)]
  transfers between devices with their start and end apart: 5 -> 11, of which waited for: 3 -> 8; matrix products, arithmetic and copies ran while one was open for 6% -> 6% of each run, Pallas kernels for 0% -> 0%
where the time goes in v2:
time: 77.5 us; the launch traced here: 77.1 us
  waiting for transfers between devices  33.3 us (43%)
  starting transfers between devices  23.5 us (30%)
  Pallas kernels  14.4 us (19%)
  local copies, waits for them, and re-layouts  4.28 us (6%)
  other arithmetic  0.8 us (1%)
    all_to_all x1, waiting for transfers between devices, local(): lax.all_to_all(packed, shard_axes, split_axis=0, concat_axis=0, tiled=True)  15.6 us
    ppermute x6, waiting for transfers between devices, exchange(): lax.ppermute(parts[k], axis, [(i, i ^ k) for i in range(count)])  12.6 us
    pallas_call x1, Pallas kernels, local(): pl.pallas_call(functools.partial(train_kernel, shards, cap, block, held,...  9.85 us
    ppermute x6, starting transfers between devices, exchange(): lax.ppermute(parts[k], axis, [(i, i ^ k) for i in range(count)])  9.54 us
    all_to_all x1, starting transfers between devices, local(): lax.all_to_all(packed, shard_axes, split_axis=0, concat_axis=0, tiled=True)  7.35 us
    all_to_all x1, starting transfers between devices, local(): lax.all_to_all(user_part, shard_axes, split_axis=0, concat_axis=0, tiled=...  5.49 us
    ppermute x1, waiting for transfers between devices, local(): other = lax.ppermute(mine, 'y', swap)  3.18 us
    unnamed x4, local copies, waits for them, and re-layouts  3.08 us
  transfers between devices with their start and end apart: 11, of which 8 were waited for; matrix products, arithmetic and copies ran while one was open for 6% of the time, Pallas kernels for 0%

profile of v2, /device:TPU:0, one launch (start us, length us, event | category | flops | bytes accessed | tf_op | source)
XLA Modules:
  0.0 77.1 jit_solution(3883645131119232495)
XLA Ops:
  0.6 2.6 %pack.1 = bf16[384,1024]{1,0:T(8,128)(2,1)} custom-call(bf16[128,1024]{1,0:T(8,128)(2,1)} %x_ref.1, s32[1,128]{1,0:T(1,128)} %bitcast.15, s32[1,128]{1,0:T(1,128)} %bitcast.16, s32[2,128]{1,0:T(2,128)} %bitcast.14, bf16[4,1024]{1,0:T(4,128)(2,1)} %user_ref.1, bf16[4,64]{1,0:T(4,128)(2,1)} %gate_ref.1), custom_call_target="tpu_custom_call" | custom-call | tf_op jit(solution)/shard_map/pack/pallas_call | solution.py:302
  3.3 7.3 %all-to-all-start = ((bf16[16,24,1024]{2,1,0:T(8,128)(2,1)}), bf16[16,24,1024]{2,1,0:T(8,128)(2,1)S(1)}, u32[]{:S(2)}, u32[]{:S(2)}) async-start(bf16[16,24,1024]{2,1,0:T(8,128)(2,1)} %bitcast.13), calls=%async_computation | async-start | bytes 1572864 | tf_op jit(solution)/shard_map/all_to_all | solution.py:308
  10.7 2.9 %copy.12 = bf16[1024,1024]{0,1:T(8,128)(2,1)S(1)} copy(bf16[1024,1024]{1,0:T(8,128)(2,1)} %param.9) | data formatting | bytes 4194304 | tf_op args[1]
  13.7 15.6 %all-to-all-done = bf16[16,24,1024]{2,1,0:T(8,128)(2,1)S(1)} async-done(((bf16[16,24,1024]{2,1,0:T(8,128)(2,1)}), bf16[16,24,1024]{2,1,0:T(8,128)(2,1)S(1)}, u32[]{:S(2)}, u32[]{:S(2)}) %all-to-all-start) | async-done | bytes 786464 | tf_op jit(solution)/shard_map/all_to_all | solution.py:308
  29.3 9.9 %train.1 = (f32[128,1024]{1,0:T(8,128)}, f32[16,40,128]{2,1,0:T(8,128)}, bf16[512,256]{1,0:T(8,128)(2,1)S(1)}, bf16[512,256]{1,0:T(8,128)(2,1)}, bf16[1024,256]{1,0:T(8,128)(2,1)}) custom-call(s32[1]{0:T(128)} %bitcast.2.core_ref, bf16[384,1024]{1,0:T(8,128)(2,1)S(1)} %bitcast.11, bf16[1024,1024]{1,0:T(8,128)(2,1)S(1)} %bitcast.10, ...), custom_call_target="tpu_custom_call" | custom-call | tf_op jit(solution)/shard_map/train/pallas_call | solution.py:321
  39.2 0.3 collective-permute-start.1
  39.7 2.0 %collective-permute-done.x_far_ref = bf16[512,256]{1,0:T(8,128)(2,1)S(1)} collective-permute-done((bf16[512,256]{1,0:T(8,128)(2,1)}, bf16[512,256]{1,0:T(8,128)(2,1)S(1)}, u32[]{:S(2)}, u32[]{:S(2)}) %collective-permute-start) | collective-permute-done | bytes 262176 | tf_op jit(solution)/shard_map/ppermute | solution.py:346
  41.7 1.8 %tower.1 = (bf16[256,512]{1,0:T(8,128)(2,1)S(1)}, bf16[256,512]{1,0:T(8,128)(2,1)S(1)}, bf16[256,512]{1,0:T(8,128)(2,1)S(1)}, bf16[256,512]{1,0:T(8,128)(2,1)S(1)}) custom-call(s32[1]{0:T(128)} %bitcast.1.me_ref, bf16[512,256]{1,0:T(8,128)(2,1)S(1)} %get-tuple-element.17.x_ref, bf16[512,256]{1,0:T(8,128)(2,1)S(1)} %collective-permute-done.x_far_ref, ...), custom_call_target="tpu_custom_call" | custom-call | tf_op jit(solution)/shard_map/tower/pallas_call | solution.py:350
  43.5 1.6 %collective-permute-start.2 = (bf16[256,512]{1,0:T(8,128)(2,1)S(1)}, bf16[256,512]{1,0:T(8,128)(2,1)S(1)}, u32[]{:S(2)}, u32[]{:S(2)}) collective-permute-start(bf16[256,512]{1,0:T(8,128)(2,1)S(1)} %get-tuple-element.21), channel_id=1, source_target_pairs={{0,2},{2,0},{16,18},{18,16},{1,3},{3,1},{17,19},{19,17},{4,6},{6,4... | collective-permute-start | bytes 786440 | tf_op jit(solution)/shard_map/ppermute | solution.py:258
  45.1 1.5 %collective-permute-start.3 = (bf16[256,512]{1,0:T(8,128)(2,1)S(1)}, bf16[256,512]{1,0:T(8,128)(2,1)S(1)}, u32[]{:S(2)}, u32[]{:S(2)}) collective-permute-start(bf16[256,512]{1,0:T(8,128)(2,1)S(1)} %get-tuple-element.22), channel_id=1, source_target_pairs={{0,16},{2,18},{16,0},{18,2},{1,17},{3,19},{17,1},{19,3},{4,20},{6,... | collective-permute-start | bytes 786440 | tf_op jit(solution)/shard_map/ppermute | solution.py:258
  46.6 0.4 collective-permute-start.4
  47.0 5.5 %all-to-all-start.1 = ((f32[16,40,128]{2,1,0:T(8,128)}), f32[16,40,128]{2,1,0:T(8,128)S(1)}, u32[]{:S(2)}, u32[]{:S(2)}) async-start(f32[16,40,128]{2,1,0:T(8,128)} %get-tuple-element.29), calls=%async_computation.1 | async-start | bytes 655360 | tf_op jit(solution)/shard_map/all_to_all | solution.py:379
  52.7 5.4 %collective-permute-done.3.refs_2_ = bf16[256,512]{1,0:T(8,128)(2,1)S(1)} collective-permute-done((bf16[256,512]{1,0:T(8,128)(2,1)S(1)}, bf16[256,512]{1,0:T(8,128)(2,1)S(1)}, u32[]{:S(2)}, u32[]{:S(2)}) %collective-permute-start.3) | collective-permute-done | bytes 262176 | tf_op jit(solution)/shard_map/ppermute | solution.py:258
  58.1 2.4 %collective-permute-done.4.refs_3_ = bf16[256,512]{1,0:T(8,128)(2,1)S(1)} collective-permute-done((bf16[256,512]{1,0:T(8,128)(2,1)S(1)}, bf16[256,512]{1,0:T(8,128)(2,1)S(1)}, u32[]{:S(2)}, u32[]{:S(2)}) %collective-permute-start.4) | collective-permute-done | bytes 262176 | tf_op jit(solution)/shard_map/ppermute | solution.py:258
  60.5 3.6 %collective-permute-start.5 = (bf16[64,512]{1,0:T(8,128)(2,1)S(1)}, bf16[64,512]{1,0:T(8,128)(2,1)S(1)}, u32[]{:S(2)}, u32[]{:S(2)}) collective-permute-start(bf16[64,512]{1,0:T(8,128)(2,1)S(1)} %get-tuple-element.25), channel_id=1, source_target_pairs={{0,4},{4,0},{8,12},{12,8},{1,5},{5,1},{9,13},{13,9},{2,6},{6,2},{1... | collective-permute-start | bytes 196616 | tf_op jit(solution)/shard_map/ppermute | solution.py:258
  64.1 1.0 %collective-permute-start.6 = (bf16[64,512]{1,0:T(8,128)(2,1)S(1)}, bf16[64,512]{1,0:T(8,128)(2,1)S(1)}, u32[]{:S(2)}, u32[]{:S(2)}) collective-permute-start(bf16[64,512]{1,0:T(8,128)(2,1)S(1)} %get-tuple-element.26), channel_id=1, source_target_pairs={{0,8},{4,12},{8,0},{12,4},{1,9},{5,13},{9,1},{13,5},{2,10},{6,14},... | collective-permute-start | bytes 196616 | tf_op jit(solution)/shard_map/ppermute | solution.py:258
  65.1 1.5 %collective-permute-start.7 = (bf16[64,512]{1,0:T(8,128)(2,1)S(1)}, bf16[64,512]{1,0:T(8,128)(2,1)S(1)}, u32[]{:S(2)}, u32[]{:S(2)}) collective-permute-start(bf16[64,512]{1,0:T(8,128)(2,1)S(1)} %get-tuple-element.27), channel_id=1, source_target_pairs={{0,12},{4,8},{8,4},{12,0},{1,13},{5,9},{9,5},{13,1},{2,14},{6,10},... | collective-permute-start | bytes 196616 | tf_op jit(solution)/shard_map/ppermute | solution.py:258
  66.5 3.4 %collective-permute-done.6 = bf16[64,512]{1,0:T(8,128)(2,1)S(1)} collective-permute-done((bf16[64,512]{1,0:T(8,128)(2,1)S(1)}, bf16[64,512]{1,0:T(8,128)(2,1)S(1)}, u32[]{:S(2)}, u32[]{:S(2)}) %collective-permute-start.6) | collective-permute-done | bytes 65568 | tf_op jit(solution)/shard_map/ppermute | solution.py:258
  70.0 1.3 %collective-permute-done.7 = bf16[64,512]{1,0:T(8,128)(2,1)S(1)} collective-permute-done((bf16[64,512]{1,0:T(8,128)(2,1)S(1)}, bf16[64,512]{1,0:T(8,128)(2,1)S(1)}, u32[]{:S(2)}, u32[]{:S(2)}) %collective-permute-start.7) | collective-permute-done | bytes 65568 | tf_op jit(solution)/shard_map/ppermute | solution.py:258
  71.3 0.6 collective-permute-start.8
  71.9 0.6 slice.9
  72.5 0.6 reshape.29
  73.1 3.2 %collective-permute-done.8 = f32[64,512]{1,0:T(8,128)S(1)} collective-permute-done((f32[64,512]{1,0:T(8,128)S(1)}, f32[64,512]{1,0:T(8,128)S(1)}, u32[]{:S(2)}, u32[]{:S(2)}) %collective-permute-start.8) | collective-permute-done | bytes 131104 | tf_op jit(solution)/shard_map/ppermute | solution.py:371
  76.3 0.7 pad_maximum_fusion
  (13 shorter events, 0.8 us)
Async XLA Ops:
  3.3 26.1 %all-to-all-start = ((bf16[16,24,1024]{2,1,0:T(8,128)(2,1)}), bf16[16,24,1024]{2,1,0:T(8,128)(2,1)S(1)}, u32[]{:S(2)}, u32[]{:S(2)}) async-start(bf16[16,24,1024]{2,1,0:T(8,128)(2,1)} %bitcast.13), calls=%async_computation | async-start | bytes 1572864 | tf_op jit(solution)/shard_map/all_to_all | solution.py:308
  10.6 2.9 %copy-start = (bf16[128,1024]{1,0:T(8,128)(2,1)S(1)}, bf16[128,1024]{1,0:T(8,128)(2,1)}, u32[]{:S(2)}) copy-start(bf16[128,1024]{1,0:T(8,128)(2,1)} %param.10) | copy-start | bytes 786436
  39.2 2.5 %collective-permute-start.1 = (bf16[1024,256]{1,0:T(8,128)(2,1)}, bf16[1024,256]{1,0:T(8,128)(2,1)S(1)}, u32[]{:S(2)}, u32[]{:S(2)}) collective-permute-start(bf16[1024,256]{1,0:T(8,128)(2,1)} %get-tuple-element.19.d_ref), channel_id=1, source_target_pairs={{0,1},{1,0},{2,3},{3,2},{4,5},{5,4},{6,7},{7,6},{8,9},{9,8},{10,11... | collective-permute-start | bytes 1572872 | tf_op jit(solution)/shard_map/ppermute | solution.py:347
  39.5 2.2 %collective-permute-start = (bf16[512,256]{1,0:T(8,128)(2,1)}, bf16[512,256]{1,0:T(8,128)(2,1)S(1)}, u32[]{:S(2)}, u32[]{:S(2)}) collective-permute-start(bf16[512,256]{1,0:T(8,128)(2,1)} %get-tuple-element.18), channel_id=1, source_target_pairs={{0,1},{1,0},{2,3},{3,2},{4,5},{5,4},{6,7},{7,6},{8,9},{9,8},{10,11... | collective-permute-start | bytes 786440 | tf_op jit(solution)/shard_map/ppermute | solution.py:346
  43.5 9.2 %collective-permute-start.2 = (bf16[256,512]{1,0:T(8,128)(2,1)S(1)}, bf16[256,512]{1,0:T(8,128)(2,1)S(1)}, u32[]{:S(2)}, u32[]{:S(2)}) collective-permute-start(bf16[256,512]{1,0:T(8,128)(2,1)S(1)} %get-tuple-element.21), channel_id=1, source_target_pairs={{0,2},{2,0},{16,18},{18,16},{1,3},{3,1},{17,19},{19,17},{4,6},{6,4... | collective-permute-start | bytes 786440 | tf_op jit(solution)/shard_map/ppermute | solution.py:258
  45.1 13.0 %collective-permute-start.3 = (bf16[256,512]{1,0:T(8,128)(2,1)S(1)}, bf16[256,512]{1,0:T(8,128)(2,1)S(1)}, u32[]{:S(2)}, u32[]{:S(2)}) collective-permute-start(bf16[256,512]{1,0:T(8,128)(2,1)S(1)} %get-tuple-element.22), channel_id=1, source_target_pairs={{0,16},{2,18},{16,0},{18,2},{1,17},{3,19},{17,1},{19,3},{4,20},{6,... | collective-permute-start | bytes 786440 | tf_op jit(solution)/shard_map/ppermute | solution.py:258
  46.6 13.8 %collective-permute-start.4 = (bf16[256,512]{1,0:T(8,128)(2,1)S(1)}, bf16[256,512]{1,0:T(8,128)(2,1)S(1)}, u32[]{:S(2)}, u32[]{:S(2)}) collective-permute-start(bf16[256,512]{1,0:T(8,128)(2,1)S(1)} %get-tuple-element.23), channel_id=1, source_target_pairs={{0,18},{2,16},{16,2},{18,0},{1,19},{3,17},{17,3},{19,1},{4,22},{6,... | collective-permute-start | bytes 786440 | tf_op jit(solution)/shard_map/ppermute | solution.py:258
  47.0 24.9 %all-to-all-start.1 = ((f32[16,40,128]{2,1,0:T(8,128)}), f32[16,40,128]{2,1,0:T(8,128)S(1)}, u32[]{:S(2)}, u32[]{:S(2)}) async-start(f32[16,40,128]{2,1,0:T(8,128)} %get-tuple-element.29), calls=%async_computation.1 | async-start | bytes 655360 | tf_op jit(solution)/shard_map/all_to_all | solution.py:379
  60.5 6.0 %collective-permute-start.5 = (bf16[64,512]{1,0:T(8,128)(2,1)S(1)}, bf16[64,512]{1,0:T(8,128)(2,1)S(1)}, u32[]{:S(2)}, u32[]{:S(2)}) collective-permute-start(bf16[64,512]{1,0:T(8,128)(2,1)S(1)} %get-tuple-element.25), channel_id=1, source_target_pairs={{0,4},{4,0},{8,12},{12,8},{1,5},{5,1},{9,13},{13,9},{2,6},{6,2},{1... | collective-permute-start | bytes 196616 | tf_op jit(solution)/shard_map/ppermute | solution.py:258
  64.1 5.9 %collective-permute-start.6 = (bf16[64,512]{1,0:T(8,128)(2,1)S(1)}, bf16[64,512]{1,0:T(8,128)(2,1)S(1)}, u32[]{:S(2)}, u32[]{:S(2)}) collective-permute-start(bf16[64,512]{1,0:T(8,128)(2,1)S(1)} %get-tuple-element.26), channel_id=1, source_target_pairs={{0,8},{4,12},{8,0},{12,4},{1,9},{5,13},{9,1},{13,5},{2,10},{6,14},... | collective-permute-start | bytes 196616 | tf_op jit(solution)/shard_map/ppermute | solution.py:258
  65.1 6.2 %collective-permute-start.7 = (bf16[64,512]{1,0:T(8,128)(2,1)S(1)}, bf16[64,512]{1,0:T(8,128)(2,1)S(1)}, u32[]{:S(2)}, u32[]{:S(2)}) collective-permute-start(bf16[64,512]{1,0:T(8,128)(2,1)S(1)} %get-tuple-element.27), channel_id=1, source_target_pairs={{0,12},{4,8},{8,4},{12,0},{1,13},{5,9},{9,5},{13,1},{2,14},{6,10},... | collective-permute-start | bytes 196616 | tf_op jit(solution)/shard_map/ppermute | solution.py:258
  71.3 5.0 %collective-permute-start.8 = (f32[64,512]{1,0:T(8,128)S(1)}, f32[64,512]{1,0:T(8,128)S(1)}, u32[]{:S(2)}, u32[]{:S(2)}) collective-permute-start(f32[64,512]{1,0:T(8,128)S(1)} %convert_add_fusion), channel_id=1, source_target_pairs={{0,16},{16,0},{1,17},{17,1},{2,18},{18,2},{3,19},{19,3},{4,20},{20... | collective-permute-start | bytes 393224 | tf_op jit(solution)/shard_map/ppermute | solution.py:371

commit v3 on v2

--- a/solution.py
+++ b/solution.py
@@ -109,7 +109,8 @@
     shards, cap, block, held, order,
     core_ref, recv_ref, wt_ref, table_t_ref,
     table_grad_ref, user_ref, x_own_ref, x_far_ref, dpt_ref,
-    comp_ref, pos_ref, neg_ref, dpos_ref, dneg_ref, norm_ref, pre_ref, scale_ref,
+    comp_ref, pos_ref, neg_ref, dpos_ref, dneg_ref, norm_ref, slope_ref, scale_ref,
+    split_ref, dense_ref, dc_ref, low_ref,
 ):
     rows, width = recv_ref.shape
     slots = shards * cap
@@ -124,8 +125,8 @@
         picked = iota((count, rows), 1) == quotient * block + first + rest
         return picked.astype(F32).astype(BF16)
 
-    x_rows = nn(rows_of(slots, cap, 0), recv)
-    x_t = jnp.transpose(x_rows).astype(BF16)
+    picked = nn(jnp.concatenate([rows_of(slots, cap, 0), rows_of(users, held, cap)], axis=0), recv)
+    x_t = jnp.transpose(picked[:slots].astype(BF16))
     unit = width // shards
     first_core = core_ref[0] == 0
     for place, (here, there) in enumerate(order):
@@ -134,7 +135,7 @@
         two = x_t[there * unit : (there + 1) * unit, :]
         x_own_ref[into, :] = jnp.where(first_core, one, two)
         x_far_ref[into, :] = jnp.where(first_core, two, one)
-    user_rows = nn(rows_of(users, held, cap), recv)
+    user_rows = picked[slots:]
     for p in range(comps):
         comp_ref[pl.ds(p, users, stride=comps), :] = user_rows[:, p * size : (p + 1) * size]
     comp_rows = comp_ref[...].astype(BF16)
@@ -169,19 +170,22 @@
     is_pos = ids3 == pos_row[None]
     is_neg = ids3 == neg_row[None]
 
+    slope_ref[...] = nn(wt_ref[...], x_t)
+    norm_ref[...] = nn(table_t_ref[...], pick_table)
     for q in range(comps):
-        part = slice(q * size, (q + 1) * size)
-        pre = nn(wt_ref[part, :], x_t)
-        pre_ref[part, :] = pre
-        embedded = (0.5 * pre * (1.0 + erf(pre * math.sqrt(0.5)))).astype(BF16).astype(F32)
-        combined = embedded + nn(table_t_ref[part, :], pick_table)
+        part, wide = slice(q * size, (q + 1) * size), slice(q * slots, (q + 1) * slots)
+        pre = slope_ref[part, :]
+        share = 0.5 + 0.5 * erf(pre * math.sqrt(0.5))
+        slope_ref[part, :] = share + pre * (jnp.exp(-0.5 * pre * pre) * (1.0 / math.sqrt(2.0 * math.pi)))
+        combined = (pre * share).astype(BF16).astype(F32) + norm_ref[part, :]
         scale = lax.rsqrt(jnp.mean(combined * combined, axis=0, keepdims=True) + 1e-06)
         scale_ref[q : q + 1, :] = scale
         normed = combined * scale
         norm_ref[part, :] = normed
         high, low = halves(normed)
-        logits = nn(comp_twice, jnp.concatenate([high, low], axis=0))
-        logits = logits.reshape(users, comps, slots)
+        split_ref[:size, wide] = high
+        split_ref[size:, wide] = low
+        logits = nn(comp_twice, split_ref[:, wide]).reshape(users, comps, slots)
         pos_ref[q * comps : (q + 1) * comps, :] = jnp.sum(jnp.where(is_pos, logits, 0.0), axis=0)
         neg_ref[q * comps : (q + 1) * comps, :] = jnp.sum(jnp.where(is_neg, logits, 0.0), axis=0)
 
@@ -197,7 +201,7 @@
     dpos_ref[...] = d_pos
     dneg_ref[...] = d_neg
 
-    pad = -(-held // 8) * 8
+    pad = user_ref.shape[1] - held * comps
     mate, rest = split_by(iota((shards * pad, slots), 0), pad)
     person = jnp.where(rest < held, mate * held + rest, -1)
     mask_pos = (person == pos_row).astype(F32).astype(BF16)
@@ -207,34 +211,31 @@
         for piece in halves(values):
             d_gate = d_gate + nt(mask, nn(swap, piece).astype(BF16))
     own = held * comps
-    user_ref[:, own:, : comps * comps] = d_gate.reshape(shards, pad, comps * comps)
+    user_ref[:, own:, : comps * comps] = d_gate.reshape(shards, pad, comps * comps).astype(BF16)
     user_ref[:, own:, comps * comps :] = jnp.zeros(
-        (shards, pad, size - comps * comps), F32
+        (shards, pad, size - comps * comps), BF16
     )
 
-    d_users = jnp.zeros((users * comps, size), F32)
     for q in range(comps):
-        part = slice(q * size, (q + 1) * size)
+        wide = slice(q * slots, (q + 1) * slots)
         d_logit_pos = dpos_ref[q * comps : (q + 1) * comps, :][None]
         d_logit_neg = dneg_ref[q * comps : (q + 1) * comps, :][None]
         dense = jnp.where(is_pos, d_logit_pos, 0.0) + jnp.where(is_neg, d_logit_neg, 0.0)
         dense_high, dense_low = halves(dense.reshape(users * comps, slots))
+        dense_ref[:, wide] = dense_high
+        part = slice(q * size, (q + 1) * size)
         normed = norm_ref[part, :]
-        high, low = halves(normed)
-        d_users = d_users + nt(dense_high, high) + nt(dense_high, low) + nt(dense_low, high)
         d_normed = nn(comp_t, dense_high) + nn(comp_t, dense_low)
         inner = jnp.mean(d_normed * normed, axis=0, keepdims=True)
         d_combined = scale_ref[q : q + 1, :] * (d_normed - normed * inner)
-        total = jnp.zeros((tables, size), F32)
-        for piece in halves(d_combined):
-            total = total + nt(pick_table, piece)
-        table_grad_ref[:, part] = total
-        pre = pre_ref[part, :]
-        slope = 0.5 * (1.0 + erf(pre * math.sqrt(0.5))) + pre * (
-            jnp.exp(-0.5 * pre * pre) * (1.0 / math.sqrt(2.0 * math.pi))
-        )
-        dpt_ref[part, :] = (d_combined.astype(BF16).astype(F32) * slope).astype(BF16)
-    user_ref[:, :own, :] = d_users.reshape(shards, own, size)
+        d_embedded = d_combined.astype(BF16)
+        dpt_ref[part, :] = (d_embedded.astype(F32) * slope_ref[part, :]).astype(BF16)
+        dc_ref[part, :] = d_embedded
+        low_ref[part, :] = (d_combined - d_embedded.astype(F32)).astype(BF16)
+    d_users = nt(dense_ref[...], split_ref[...])
+    d_users = d_users[:, :size] + d_users[:, size:]
+    user_ref[:, :own, :] = d_users.reshape(shards, own, size).astype(BF16)
+    table_grad_ref[...] = nt(pick_table, dc_ref[...]) + nt(pick_table, low_ref[...])
 
 
 def views(refs, count):
@@ -317,12 +318,12 @@
     scalar = pl.BlockSpec(memory_space=pltpu.SMEM)
     vmem = pl.BlockSpec(memory_space=pltpu.VMEM)
     own = held * COMPS
-    pad = -(-held // 8) * 8
+    pad = -(-held // 16) * 16
     table_grad, user_part, x_own, x_send, dp_t = pl.pallas_call(
         functools.partial(train_kernel, shards, cap, block, held, order),
         out_shape=(
             jax.ShapeDtypeStruct((item_table.shape[0], width), F32),
-            jax.ShapeDtypeStruct((shards, own + pad, size), F32),
+            jax.ShapeDtypeStruct((shards, own + pad, size), BF16),
             jax.ShapeDtypeStruct((half, slots), BF16),
             jax.ShapeDtypeStruct((half, slots), BF16),
             jax.ShapeDtypeStruct((width, slots), BF16),
@@ -337,6 +338,10 @@
             pltpu.VMEM((width, slots), F32),
             pltpu.VMEM((width, slots), F32),
             pltpu.VMEM((COMPS, slots), F32),
+            pltpu.VMEM((2 * size, COMPS * slots), BF16),
+            pltpu.VMEM((users * COMPS, COMPS * slots), BF16),
+            pltpu.VMEM((width, slots), BF16),
+            pltpu.VMEM((width, slots), BF16),
         ],
         compiler_params=params,
         name="train",
@@ -377,7 +382,7 @@
         tower_grad = lax.all_gather(mine, "y", axis=1, tiled=True)
 
     got_users = lax.all_to_all(user_part, shard_axes, split_axis=0, concat_axis=0, tiled=True)
-    user_sum = jnp.sum(got_users, axis=0)
+    user_sum = jnp.sum(got_users.astype(F32), axis=0)
     user_comp_grad = user_sum[:own].reshape(held, width)
     user_gate_grad = user_sum[own : own + held, : COMPS * COMPS]
     return tower_grad, table_grad, user_comp_grad, user_gate_grad

time: 77.5 us -> 74.4 us (0.960)
  Pallas kernels: 14.4 us -> 11.4 us
    pallas_call x1, Pallas kernels: 9.85 us -> 6.84 us  [local(): pl.pallas_call(functools.partial(train_kernel, shards, cap, block, held,...]
    unnamed x4 -> x6, local copies, waits for them, and re-layouts: 3.08 us -> 3.75 us
  transfers between devices with their start and end apart: 11 -> 11, of which waited for: 8 -> 7; matrix products, arithmetic and copies ran while one was open for 6% -> 6% of each run, Pallas kernels for 0% -> 0%
where the time goes in v3:
time: 74.4 us; the launch traced here: 73.9 us
  waiting for transfers between devices  32.8 us (44%)
  starting transfers between devices  23.3 us (31%)
  Pallas kernels  11.4 us (15%)
  local copies, waits for them, and re-layouts  4.95 us (7%)
  other arithmetic  0.81 us (1%)
    all_to_all x1, waiting for transfers between devices, local(): lax.all_to_all(packed, shard_axes, split_axis=0, concat_axis=0, tiled=True)  15.6 us
    ppermute x6, waiting for transfers between devices, exchange(): lax.ppermute(parts[k], axis, [(i, i ^ k) for i in range(count)])  12 us
    ppermute x6, starting transfers between devices, exchange(): lax.ppermute(parts[k], axis, [(i, i ^ k) for i in range(count)])  9.34 us
    all_to_all x1, starting transfers between devices, local(): lax.all_to_all(packed, shard_axes, split_axis=0, concat_axis=0, tiled=True)  7.35 us
    pallas_call x1, Pallas kernels, local(): pl.pallas_call(functools.partial(train_kernel, shards, cap, block, held,...  6.84 us
    all_to_all x1, starting transfers between devices, local(): lax.all_to_all(user_part, shard_axes, split_axis=0, concat_axis=0, tiled=...  5.47 us
    unnamed x6, local copies, waits for them, and re-layouts  3.75 us
    ppermute x1, waiting for transfers between devices, local(): other = lax.ppermute(mine, 'y', swap)  3.18 us
  transfers between devices with their start and end apart: 11, of which 7 were waited for; matrix products, arithmetic and copies ran while one was open for 6% of the time, Pallas kernels for 0%

profile of v3, /device:TPU:0, one launch (start us, length us, event | category | flops | bytes accessed | tf_op | source)
XLA Modules:
  0.0 73.9 jit_solution(2369714523219240971)
XLA Ops:
  0.6 2.6 %pack.1 = bf16[384,1024]{1,0:T(8,128)(2,1)} custom-call(bf16[128,1024]{1,0:T(8,128)(2,1)} %x_ref.1, s32[1,128]{1,0:T(1,128)} %bitcast.15, s32[1,128]{1,0:T(1,128)} %bitcast.16, s32[2,128]{1,0:T(2,128)} %bitcast.14, bf16[4,1024]{1,0:T(4,128)(2,1)} %user_ref.1, bf16[4,64]{1,0:T(4,128)(2,1)} %gate_ref.1), custom_call_target="tpu_custom_call" | custom-call | tf_op jit(solution)/shard_map/pack/pallas_call | solution.py:303
  3.3 7.3 %all-to-all-start = ((bf16[16,24,1024]{2,1,0:T(8,128)(2,1)}), bf16[16,24,1024]{2,1,0:T(8,128)(2,1)S(1)}, u32[]{:S(2)}, u32[]{:S(2)}) async-start(bf16[16,24,1024]{2,1,0:T(8,128)(2,1)} %bitcast.13), calls=%async_computation | async-start | bytes 1572864 | tf_op jit(solution)/shard_map/all_to_all | solution.py:309
  10.6 2.9 %copy.12 = bf16[1024,1024]{0,1:T(8,128)(2,1)S(1)} copy(bf16[1024,1024]{1,0:T(8,128)(2,1)} %param.9) | data formatting | bytes 4194304 | tf_op args[1]
  13.7 15.6 %all-to-all-done = bf16[16,24,1024]{2,1,0:T(8,128)(2,1)S(1)} async-done(((bf16[16,24,1024]{2,1,0:T(8,128)(2,1)}), bf16[16,24,1024]{2,1,0:T(8,128)(2,1)S(1)}, u32[]{:S(2)}, u32[]{:S(2)}) %all-to-all-start) | async-done | bytes 786464 | tf_op jit(solution)/shard_map/all_to_all | solution.py:309
  29.3 6.8 %train.1 = (f32[128,1024]{1,0:T(8,128)}, bf16[16,48,128]{2,1,0:T(8,128)(2,1)S(1)}, bf16[512,256]{1,0:T(8,128)(2,1)S(1)}, bf16[512,256]{1,0:T(8,128)(2,1)}, bf16[1024,256]{1,0:T(8,128)(2,1)}) custom-call(s32[1]{0:T(128)} %bitcast.2.core_ref, bf16[384,1024]{1,0:T(8,128)(2,1)S(1)} %bitcast.11, bf16[1024,1024]{1,0:T(8,128)(2,1)S(1)} %bitcast.10, ...), custom_call_target="tpu_custom_call" | custom-call | tf_op jit(solution)/shard_map/train/pallas_call | solution.py:322
  36.2 0.7 copy-done
  37.1 0.3 collective-permute-start
  37.4 2.0 %collective-permute-done.x_far_ref = bf16[512,256]{1,0:T(8,128)(2,1)S(1)} collective-permute-done((bf16[512,256]{1,0:T(8,128)(2,1)}, bf16[512,256]{1,0:T(8,128)(2,1)S(1)}, u32[]{:S(2)}, u32[]{:S(2)}) %collective-permute-start) | collective-permute-done | bytes 262176 | tf_op jit(solution)/shard_map/ppermute | solution.py:351
  39.4 1.8 %tower.1 = (bf16[256,512]{1,0:T(8,128)(2,1)S(1)}, bf16[256,512]{1,0:T(8,128)(2,1)S(1)}, bf16[256,512]{1,0:T(8,128)(2,1)S(1)}, bf16[256,512]{1,0:T(8,128)(2,1)S(1)}) custom-call(s32[1]{0:T(128)} %bitcast.1.me_ref, bf16[512,256]{1,0:T(8,128)(2,1)S(1)} %get-tuple-element.17.x_ref, bf16[512,256]{1,0:T(8,128)(2,1)S(1)} %collective-permute-done.x_far_ref, ...), custom_call_target="tpu_custom_call" | custom-call | tf_op jit(solution)/shard_map/tower/pallas_call | solution.py:355
  41.1 1.6 %collective-permute-start.2 = (bf16[256,512]{1,0:T(8,128)(2,1)S(1)}, bf16[256,512]{1,0:T(8,128)(2,1)S(1)}, u32[]{:S(2)}, u32[]{:S(2)}) collective-permute-start(bf16[256,512]{1,0:T(8,128)(2,1)S(1)} %get-tuple-element.21), channel_id=1, source_target_pairs={{0,2},{2,0},{16,18},{18,16},{1,3},{3,1},{17,19},{19,17},{4,6},{6,4... | collective-permute-start | bytes 786440 | tf_op jit(solution)/shard_map/ppermute | solution.py:259
  42.7 1.5 %collective-permute-start.3 = (bf16[256,512]{1,0:T(8,128)(2,1)S(1)}, bf16[256,512]{1,0:T(8,128)(2,1)S(1)}, u32[]{:S(2)}, u32[]{:S(2)}) collective-permute-start(bf16[256,512]{1,0:T(8,128)(2,1)S(1)} %get-tuple-element.22), channel_id=1, source_target_pairs={{0,16},{2,18},{16,0},{18,2},{1,17},{3,19},{17,1},{19,3},{4,20},{6,... | collective-permute-start | bytes 786440 | tf_op jit(solution)/shard_map/ppermute | solution.py:259
  44.2 0.5 collective-permute-start.4
  44.7 5.5 %all-to-all-start.1 = ((bf16[16,48,128]{2,1,0:T(8,128)(2,1)}), bf16[16,48,128]{2,1,0:T(8,128)(2,1)S(1)}, u32[]{:S(2)}, u32[]{:S(2)}) async-start(bf16[16,48,128]{2,1,0:T(8,128)(2,1)} %copy-done), calls=%async_computation.1 | async-start | bytes 393216 | tf_op jit(solution)/shard_map/all_to_all | solution.py:384
  50.3 5.4 %collective-permute-done.3.refs_2_ = bf16[256,512]{1,0:T(8,128)(2,1)S(1)} collective-permute-done((bf16[256,512]{1,0:T(8,128)(2,1)S(1)}, bf16[256,512]{1,0:T(8,128)(2,1)S(1)}, u32[]{:S(2)}, u32[]{:S(2)}) %collective-permute-start.3) | collective-permute-done | bytes 262176 | tf_op jit(solution)/shard_map/ppermute | solution.py:259
  55.8 1.7 %collective-permute-done.4.refs_3_ = bf16[256,512]{1,0:T(8,128)(2,1)S(1)} collective-permute-done((bf16[256,512]{1,0:T(8,128)(2,1)S(1)}, bf16[256,512]{1,0:T(8,128)(2,1)S(1)}, u32[]{:S(2)}, u32[]{:S(2)}) %collective-permute-start.4) | collective-permute-done | bytes 262176 | tf_op jit(solution)/shard_map/ppermute | solution.py:259
  57.6 3.4 %collective-permute-start.5 = (bf16[64,512]{1,0:T(8,128)(2,1)S(1)}, bf16[64,512]{1,0:T(8,128)(2,1)S(1)}, u32[]{:S(2)}, u32[]{:S(2)}) collective-permute-start(bf16[64,512]{1,0:T(8,128)(2,1)S(1)} %get-tuple-element.25), channel_id=1, source_target_pairs={{0,4},{4,0},{8,12},{12,8},{1,5},{5,1},{9,13},{13,9},{2,6},{6,2},{1... | collective-permute-start | bytes 196616 | tf_op jit(solution)/shard_map/ppermute | solution.py:259
  61.0 1.0 %collective-permute-start.6 = (bf16[64,512]{1,0:T(8,128)(2,1)S(1)}, bf16[64,512]{1,0:T(8,128)(2,1)S(1)}, u32[]{:S(2)}, u32[]{:S(2)}) collective-permute-start(bf16[64,512]{1,0:T(8,128)(2,1)S(1)} %get-tuple-element.26), channel_id=1, source_target_pairs={{0,8},{4,12},{8,0},{12,4},{1,9},{5,13},{9,1},{13,5},{2,10},{6,14},... | collective-permute-start | bytes 196616 | tf_op jit(solution)/shard_map/ppermute | solution.py:259
  61.9 1.5 %collective-permute-start.7 = (bf16[64,512]{1,0:T(8,128)(2,1)S(1)}, bf16[64,512]{1,0:T(8,128)(2,1)S(1)}, u32[]{:S(2)}, u32[]{:S(2)}) collective-permute-start(bf16[64,512]{1,0:T(8,128)(2,1)S(1)} %get-tuple-element.27), channel_id=1, source_target_pairs={{0,12},{4,8},{8,4},{12,0},{1,13},{5,9},{9,5},{13,1},{2,14},{6,10},... | collective-permute-start | bytes 196616 | tf_op jit(solution)/shard_map/ppermute | solution.py:259
  63.4 4.7 %collective-permute-done.6 = bf16[64,512]{1,0:T(8,128)(2,1)S(1)} collective-permute-done((bf16[64,512]{1,0:T(8,128)(2,1)S(1)}, bf16[64,512]{1,0:T(8,128)(2,1)S(1)}, u32[]{:S(2)}, u32[]{:S(2)}) %collective-permute-start.6) | collective-permute-done | bytes 65568 | tf_op jit(solution)/shard_map/ppermute | solution.py:259
  68.2 0.6 collective-permute-start.8
  68.8 0.6 slice.9
  69.4 0.6 reshape.29
  70.0 3.2 %collective-permute-done.8 = f32[64,512]{1,0:T(8,128)S(1)} collective-permute-done((f32[64,512]{1,0:T(8,128)S(1)}, f32[64,512]{1,0:T(8,128)S(1)}, u32[]{:S(2)}, u32[]{:S(2)}) %collective-permute-start.8) | collective-permute-done | bytes 131104 | tf_op jit(solution)/shard_map/ppermute | solution.py:376
  73.2 0.7 pad_maximum_fusion
  (15 shorter events, 0.8 us)
Async XLA Ops:
  3.3 26.1 %all-to-all-start = ((bf16[16,24,1024]{2,1,0:T(8,128)(2,1)}), bf16[16,24,1024]{2,1,0:T(8,128)(2,1)S(1)}, u32[]{:S(2)}, u32[]{:S(2)}) async-start(bf16[16,24,1024]{2,1,0:T(8,128)(2,1)} %bitcast.13), calls=%async_computation | async-start | bytes 1572864 | tf_op jit(solution)/shard_map/all_to_all | solution.py:309
  10.6 2.9 %copy-start.1 = (bf16[128,1024]{1,0:T(8,128)(2,1)S(1)}, bf16[128,1024]{1,0:T(8,128)(2,1)}, u32[]{:S(2)}) copy-start(bf16[128,1024]{1,0:T(8,128)(2,1)} %param.10) | copy-start | bytes 786436
  36.2 0.7 copy-start
  36.9 2.5 %collective-permute-start.1 = (bf16[1024,256]{1,0:T(8,128)(2,1)}, bf16[1024,256]{1,0:T(8,128)(2,1)S(1)}, u32[]{:S(2)}, u32[]{:S(2)}) collective-permute-start(bf16[1024,256]{1,0:T(8,128)(2,1)} %get-tuple-element.19.d_ref), channel_id=1, source_target_pairs={{0,1},{1,0},{2,3},{3,2},{4,5},{5,4},{6,7},{7,6},{8,9},{9,8},{10,11... | collective-permute-start | bytes 1572872 | tf_op jit(solution)/shard_map/ppermute | solution.py:352
  37.1 2.2 %collective-permute-start = (bf16[512,256]{1,0:T(8,128)(2,1)}, bf16[512,256]{1,0:T(8,128)(2,1)S(1)}, u32[]{:S(2)}, u32[]{:S(2)}) collective-permute-start(bf16[512,256]{1,0:T(8,128)(2,1)} %get-tuple-element.18), channel_id=1, source_target_pairs={{0,1},{1,0},{2,3},{3,2},{4,5},{5,4},{6,7},{7,6},{8,9},{9,8},{10,11... | collective-permute-start | bytes 786440 | tf_op jit(solution)/shard_map/ppermute | solution.py:351
  41.1 9.2 %collective-permute-start.2 = (bf16[256,512]{1,0:T(8,128)(2,1)S(1)}, bf16[256,512]{1,0:T(8,128)(2,1)S(1)}, u32[]{:S(2)}, u32[]{:S(2)}) collective-permute-start(bf16[256,512]{1,0:T(8,128)(2,1)S(1)} %get-tuple-element.21), channel_id=1, source_target_pairs={{0,2},{2,0},{16,18},{18,16},{1,3},{3,1},{17,19},{19,17},{4,6},{6,4... | collective-permute-start | bytes 786440 | tf_op jit(solution)/shard_map/ppermute | solution.py:259
  42.7 13.1 %collective-permute-start.3 = (bf16[256,512]{1,0:T(8,128)(2,1)S(1)}, bf16[256,512]{1,0:T(8,128)(2,1)S(1)}, u32[]{:S(2)}, u32[]{:S(2)}) collective-permute-start(bf16[256,512]{1,0:T(8,128)(2,1)S(1)} %get-tuple-element.22), channel_id=1, source_target_pairs={{0,16},{2,18},{16,0},{18,2},{1,17},{3,19},{17,1},{19,3},{4,20},{6,... | collective-permute-start | bytes 786440 | tf_op jit(solution)/shard_map/ppermute | solution.py:259
  44.2 13.2 %collective-permute-start.4 = (bf16[256,512]{1,0:T(8,128)(2,1)S(1)}, bf16[256,512]{1,0:T(8,128)(2,1)S(1)}, u32[]{:S(2)}, u32[]{:S(2)}) collective-permute-start(bf16[256,512]{1,0:T(8,128)(2,1)S(1)} %get-tuple-element.23), channel_id=1, source_target_pairs={{0,18},{2,16},{16,2},{18,0},{1,19},{3,17},{17,3},{19,1},{4,22},{6,... | collective-permute-start | bytes 786440 | tf_op jit(solution)/shard_map/ppermute | solution.py:259
  44.7 24.1 %all-to-all-start.1 = ((bf16[16,48,128]{2,1,0:T(8,128)(2,1)}), bf16[16,48,128]{2,1,0:T(8,128)(2,1)S(1)}, u32[]{:S(2)}, u32[]{:S(2)}) async-start(bf16[16,48,128]{2,1,0:T(8,128)(2,1)} %copy-done), calls=%async_computation.1 | async-start | bytes 393216 | tf_op jit(solution)/shard_map/all_to_all | solution.py:384
  57.6 5.8 %collective-permute-start.5 = (bf16[64,512]{1,0:T(8,128)(2,1)S(1)}, bf16[64,512]{1,0:T(8,128)(2,1)S(1)}, u32[]{:S(2)}, u32[]{:S(2)}) collective-permute-start(bf16[64,512]{1,0:T(8,128)(2,1)S(1)} %get-tuple-element.25), channel_id=1, source_target_pairs={{0,4},{4,0},{8,12},{12,8},{1,5},{5,1},{9,13},{13,9},{2,6},{6,2},{1... | collective-permute-start | bytes 196616 | tf_op jit(solution)/shard_map/ppermute | solution.py:259
  61.0 7.2 %collective-permute-start.6 = (bf16[64,512]{1,0:T(8,128)(2,1)S(1)}, bf16[64,512]{1,0:T(8,128)(2,1)S(1)}, u32[]{:S(2)}, u32[]{:S(2)}) collective-permute-start(bf16[64,512]{1,0:T(8,128)(2,1)S(1)} %get-tuple-element.26), channel_id=1, source_target_pairs={{0,8},{4,12},{8,0},{12,4},{1,9},{5,13},{9,1},{13,5},{2,10},{6,14},... | collective-permute-start | bytes 196616 | tf_op jit(solution)/shard_map/ppermute | solution.py:259
  61.9 6.2 %collective-permute-start.7 = (bf16[64,512]{1,0:T(8,128)(2,1)S(1)}, bf16[64,512]{1,0:T(8,128)(2,1)S(1)}, u32[]{:S(2)}, u32[]{:S(2)}) collective-permute-start(bf16[64,512]{1,0:T(8,128)(2,1)S(1)} %get-tuple-element.27), channel_id=1, source_target_pairs={{0,12},{4,8},{8,4},{12,0},{1,13},{5,9},{9,5},{13,1},{2,14},{6,10},... | collective-permute-start | bytes 196616 | tf_op jit(solution)/shard_map/ppermute | solution.py:259
  68.2 5.0 %collective-permute-start.8 = (f32[64,512]{1,0:T(8,128)S(1)}, f32[64,512]{1,0:T(8,128)S(1)}, u32[]{:S(2)}, u32[]{:S(2)}) collective-permute-start(f32[64,512]{1,0:T(8,128)S(1)} %convert_add_fusion), channel_id=1, source_target_pairs={{0,16},{16,0},{1,17},{17,1},{2,18},{18,2},{3,19},{19,3},{4,20},{20... | collective-permute-start | bytes 393224 | tf_op jit(solution)/shard_map/ppermute | solution.py:376

commit v4 on v3

--- a/solution.py
+++ b/solution.py
@@ -14,7 +14,7 @@
 LANES = 128
 F32 = jnp.float32
 BF16 = jnp.bfloat16
-VMEM_LIMIT = 48 * 1024 * 1024
+VMEM_LIMIT = 24 * 1024 * 1024
 PACK_LIMIT = 60 * 1024 * 1024
 FEW = 4
 

time: 74.4 us -> 74.4 us (level)
  no operation moved by 1% of the time
where the time goes in v4:
time: 74.4 us; the launch traced here: 73.9 us
  waiting for transfers between devices  32.8 us (44%)
  starting transfers between devices  23.3 us (31%)
  Pallas kernels  11.4 us (15%)
  local copies, waits for them, and re-layouts  4.95 us (7%)
  other arithmetic  0.81 us (1%)
    all_to_all x1, waiting for transfers between devices, local(): lax.all_to_all(packed, shard_axes, split_axis=0, concat_axis=0, tiled=True)  15.6 us
    ppermute x6, waiting for transfers between devices, exchange(): lax.ppermute(parts[k], axis, [(i, i ^ k) for i in range(count)])  12 us
    ppermute x6, starting transfers between devices, exchange(): lax.ppermute(parts[k], axis, [(i, i ^ k) for i in range(count)])  9.34 us
    all_to_all x1, starting transfers between devices, local(): lax.all_to_all(packed, shard_axes, split_axis=0, concat_axis=0, tiled=True)  7.35 us
    pallas_call x1, Pallas kernels, local(): pl.pallas_call(functools.partial(train_kernel, shards, cap, block, held,...  6.84 us
    all_to_all x1, starting transfers between devices, local(): lax.all_to_all(user_part, shard_axes, split_axis=0, concat_axis=0, tiled=...  5.47 us
    unnamed x6, local copies, waits for them, and re-layouts  3.75 us
    ppermute x1, waiting for transfers between devices, local(): other = lax.ppermute(mine, 'y', swap)  3.18 us
  transfers between devices with their start and end apart: 11, of which 7 were waited for; matrix products, arithmetic and copies ran while one was open for 6% of the time, Pallas kernels for 0%

profile of v4, /device:TPU:0, one launch (start us, length us, event | category | flops | bytes accessed | tf_op | source)
XLA Modules:
  0.0 73.9 jit_solution(14870885009848447656)
XLA Ops:
  0.6 2.6 %pack.1 = bf16[384,1024]{1,0:T(8,128)(2,1)} custom-call(bf16[128,1024]{1,0:T(8,128)(2,1)} %x_ref.1, s32[1,128]{1,0:T(1,128)} %bitcast.15, s32[1,128]{1,0:T(1,128)} %bitcast.16, s32[2,128]{1,0:T(2,128)} %bitcast.14, bf16[4,1024]{1,0:T(4,128)(2,1)} %user_ref.1, bf16[4,64]{1,0:T(4,128)(2,1)} %gate_ref.1), custom_call_target="tpu_custom_call" | custom-call | tf_op jit(solution)/shard_map/pack/pallas_call | solution.py:303
  3.3 7.3 %all-to-all-start = ((bf16[16,24,1024]{2,1,0:T(8,128)(2,1)}), bf16[16,24,1024]{2,1,0:T(8,128)(2,1)S(1)}, u32[]{:S(2)}, u32[]{:S(2)}) async-start(bf16[16,24,1024]{2,1,0:T(8,128)(2,1)} %bitcast.13), calls=%async_computation | async-start | bytes 1572864 | tf_op jit(solution)/shard_map/all_to_all | solution.py:309
  10.6 2.9 %copy.12 = bf16[1024,1024]{0,1:T(8,128)(2,1)S(1)} copy(bf16[1024,1024]{1,0:T(8,128)(2,1)} %param.9) | data formatting | bytes 4194304 | tf_op args[1]
  13.7 15.6 %all-to-all-done = bf16[16,24,1024]{2,1,0:T(8,128)(2,1)S(1)} async-done(((bf16[16,24,1024]{2,1,0:T(8,128)(2,1)}), bf16[16,24,1024]{2,1,0:T(8,128)(2,1)S(1)}, u32[]{:S(2)}, u32[]{:S(2)}) %all-to-all-start) | async-done | bytes 786464 | tf_op jit(solution)/shard_map/all_to_all | solution.py:309
  29.3 6.8 %train.1 = (f32[128,1024]{1,0:T(8,128)}, bf16[16,48,128]{2,1,0:T(8,128)(2,1)S(1)}, bf16[512,256]{1,0:T(8,128)(2,1)S(1)}, bf16[512,256]{1,0:T(8,128)(2,1)}, bf16[1024,256]{1,0:T(8,128)(2,1)}) custom-call(s32[1]{0:T(128)} %bitcast.2.core_ref, bf16[384,1024]{1,0:T(8,128)(2,1)S(1)} %bitcast.11, bf16[1024,1024]{1,0:T(8,128)(2,1)S(1)} %bitcast.10, ...), custom_call_target="tpu_custom_call" | custom-call | tf_op jit(solution)/shard_map/train/pallas_call | solution.py:322
  36.2 0.7 copy-done
  37.1 0.3 collective-permute-start
  37.4 2.0 %collective-permute-done.x_far_ref = bf16[512,256]{1,0:T(8,128)(2,1)S(1)} collective-permute-done((bf16[512,256]{1,0:T(8,128)(2,1)}, bf16[512,256]{1,0:T(8,128)(2,1)S(1)}, u32[]{:S(2)}, u32[]{:S(2)}) %collective-permute-start) | collective-permute-done | bytes 262176 | tf_op jit(solution)/shard_map/ppermute | solution.py:351
  39.4 1.8 %tower.1 = (bf16[256,512]{1,0:T(8,128)(2,1)S(1)}, bf16[256,512]{1,0:T(8,128)(2,1)S(1)}, bf16[256,512]{1,0:T(8,128)(2,1)S(1)}, bf16[256,512]{1,0:T(8,128)(2,1)S(1)}) custom-call(s32[1]{0:T(128)} %bitcast.1.me_ref, bf16[512,256]{1,0:T(8,128)(2,1)S(1)} %get-tuple-element.17.x_ref, bf16[512,256]{1,0:T(8,128)(2,1)S(1)} %collective-permute-done.x_far_ref, ...), custom_call_target="tpu_custom_call" | custom-call | tf_op jit(solution)/shard_map/tower/pallas_call | solution.py:355
  41.1 1.6 %collective-permute-start.2 = (bf16[256,512]{1,0:T(8,128)(2,1)S(1)}, bf16[256,512]{1,0:T(8,128)(2,1)S(1)}, u32[]{:S(2)}, u32[]{:S(2)}) collective-permute-start(bf16[256,512]{1,0:T(8,128)(2,1)S(1)} %get-tuple-element.21), channel_id=1, source_target_pairs={{0,2},{2,0},{16,18},{18,16},{1,3},{3,1},{17,19},{19,17},{4,6},{6,4... | collective-permute-start | bytes 786440 | tf_op jit(solution)/shard_map/ppermute | solution.py:259
  42.7 1.5 %collective-permute-start.3 = (bf16[256,512]{1,0:T(8,128)(2,1)S(1)}, bf16[256,512]{1,0:T(8,128)(2,1)S(1)}, u32[]{:S(2)}, u32[]{:S(2)}) collective-permute-start(bf16[256,512]{1,0:T(8,128)(2,1)S(1)} %get-tuple-element.22), channel_id=1, source_target_pairs={{0,16},{2,18},{16,0},{18,2},{1,17},{3,19},{17,1},{19,3},{4,20},{6,... | collective-permute-start | bytes 786440 | tf_op jit(solution)/shard_map/ppermute | solution.py:259
  44.2 0.5 collective-permute-start.4
  44.7 5.5 %all-to-all-start.1 = ((bf16[16,48,128]{2,1,0:T(8,128)(2,1)}), bf16[16,48,128]{2,1,0:T(8,128)(2,1)S(1)}, u32[]{:S(2)}, u32[]{:S(2)}) async-start(bf16[16,48,128]{2,1,0:T(8,128)(2,1)} %copy-done), calls=%async_computation.1 | async-start | bytes 393216 | tf_op jit(solution)/shard_map/all_to_all | solution.py:384
  50.3 5.4 %collective-permute-done.3.refs_2_ = bf16[256,512]{1,0:T(8,128)(2,1)S(1)} collective-permute-done((bf16[256,512]{1,0:T(8,128)(2,1)S(1)}, bf16[256,512]{1,0:T(8,128)(2,1)S(1)}, u32[]{:S(2)}, u32[]{:S(2)}) %collective-permute-start.3) | collective-permute-done | bytes 262176 | tf_op jit(solution)/shard_map/ppermute | solution.py:259
  55.8 1.7 %collective-permute-done.4.refs_3_ = bf16[256,512]{1,0:T(8,128)(2,1)S(1)} collective-permute-done((bf16[256,512]{1,0:T(8,128)(2,1)S(1)}, bf16[256,512]{1,0:T(8,128)(2,1)S(1)}, u32[]{:S(2)}, u32[]{:S(2)}) %collective-permute-start.4) | collective-permute-done | bytes 262176 | tf_op jit(solution)/shard_map/ppermute | solution.py:259
  57.6 3.4 %collective-permute-start.5 = (bf16[64,512]{1,0:T(8,128)(2,1)S(1)}, bf16[64,512]{1,0:T(8,128)(2,1)S(1)}, u32[]{:S(2)}, u32[]{:S(2)}) collective-permute-start(bf16[64,512]{1,0:T(8,128)(2,1)S(1)} %get-tuple-element.25), channel_id=1, source_target_pairs={{0,4},{4,0},{8,12},{12,8},{1,5},{5,1},{9,13},{13,9},{2,6},{6,2},{1... | collective-permute-start | bytes 196616 | tf_op jit(solution)/shard_map/ppermute | solution.py:259
  61.0 1.0 %collective-permute-start.6 = (bf16[64,512]{1,0:T(8,128)(2,1)S(1)}, bf16[64,512]{1,0:T(8,128)(2,1)S(1)}, u32[]{:S(2)}, u32[]{:S(2)}) collective-permute-start(bf16[64,512]{1,0:T(8,128)(2,1)S(1)} %get-tuple-element.26), channel_id=1, source_target_pairs={{0,8},{4,12},{8,0},{12,4},{1,9},{5,13},{9,1},{13,5},{2,10},{6,14},... | collective-permute-start | bytes 196616 | tf_op jit(solution)/shard_map/ppermute | solution.py:259
  61.9 1.5 %collective-permute-start.7 = (bf16[64,512]{1,0:T(8,128)(2,1)S(1)}, bf16[64,512]{1,0:T(8,128)(2,1)S(1)}, u32[]{:S(2)}, u32[]{:S(2)}) collective-permute-start(bf16[64,512]{1,0:T(8,128)(2,1)S(1)} %get-tuple-element.27), channel_id=1, source_target_pairs={{0,12},{4,8},{8,4},{12,0},{1,13},{5,9},{9,5},{13,1},{2,14},{6,10},... | collective-permute-start | bytes 196616 | tf_op jit(solution)/shard_map/ppermute | solution.py:259
  63.4 4.7 %collective-permute-done.6 = bf16[64,512]{1,0:T(8,128)(2,1)S(1)} collective-permute-done((bf16[64,512]{1,0:T(8,128)(2,1)S(1)}, bf16[64,512]{1,0:T(8,128)(2,1)S(1)}, u32[]{:S(2)}, u32[]{:S(2)}) %collective-permute-start.6) | collective-permute-done | bytes 65568 | tf_op jit(solution)/shard_map/ppermute | solution.py:259
  68.2 0.6 collective-permute-start.8
  68.8 0.6 slice.9
  69.4 0.6 reshape.29
  70.0 3.2 %collective-permute-done.8 = f32[64,512]{1,0:T(8,128)S(1)} collective-permute-done((f32[64,512]{1,0:T(8,128)S(1)}, f32[64,512]{1,0:T(8,128)S(1)}, u32[]{:S(2)}, u32[]{:S(2)}) %collective-permute-start.8) | collective-permute-done | bytes 131104 | tf_op jit(solution)/shard_map/ppermute | solution.py:376
  73.2 0.7 pad_maximum_fusion
  (15 shorter events, 0.8 us)
Async XLA Ops:
  3.3 26.1 %all-to-all-start = ((bf16[16,24,1024]{2,1,0:T(8,128)(2,1)}), bf16[16,24,1024]{2,1,0:T(8,128)(2,1)S(1)}, u32[]{:S(2)}, u32[]{:S(2)}) async-start(bf16[16,24,1024]{2,1,0:T(8,128)(2,1)} %bitcast.13), calls=%async_computation | async-start | bytes 1572864 | tf_op jit(solution)/shard_map/all_to_all | solution.py:309
  10.6 2.9 %copy-start.1 = (bf16[128,1024]{1,0:T(8,128)(2,1)S(1)}, bf16[128,1024]{1,0:T(8,128)(2,1)}, u32[]{:S(2)}) copy-start(bf16[128,1024]{1,0:T(8,128)(2,1)} %param.10) | copy-start | bytes 786436
  36.2 0.7 copy-start
  36.9 2.5 %collective-permute-start.1 = (bf16[1024,256]{1,0:T(8,128)(2,1)}, bf16[1024,256]{1,0:T(8,128)(2,1)S(1)}, u32[]{:S(2)}, u32[]{:S(2)}) collective-permute-start(bf16[1024,256]{1,0:T(8,128)(2,1)} %get-tuple-element.19.d_ref), channel_id=1, source_target_pairs={{0,1},{1,0},{2,3},{3,2},{4,5},{5,4},{6,7},{7,6},{8,9},{9,8},{10,11... | collective-permute-start | bytes 1572872 | tf_op jit(solution)/shard_map/ppermute | solution.py:352
  37.1 2.2 %collective-permute-start = (bf16[512,256]{1,0:T(8,128)(2,1)}, bf16[512,256]{1,0:T(8,128)(2,1)S(1)}, u32[]{:S(2)}, u32[]{:S(2)}) collective-permute-start(bf16[512,256]{1,0:T(8,128)(2,1)} %get-tuple-element.18), channel_id=1, source_target_pairs={{0,1},{1,0},{2,3},{3,2},{4,5},{5,4},{6,7},{7,6},{8,9},{9,8},{10,11... | collective-permute-start | bytes 786440 | tf_op jit(solution)/shard_map/ppermute | solution.py:351
  41.1 9.2 %collective-permute-start.2 = (bf16[256,512]{1,0:T(8,128)(2,1)S(1)}, bf16[256,512]{1,0:T(8,128)(2,1)S(1)}, u32[]{:S(2)}, u32[]{:S(2)}) collective-permute-start(bf16[256,512]{1,0:T(8,128)(2,1)S(1)} %get-tuple-element.21), channel_id=1, source_target_pairs={{0,2},{2,0},{16,18},{18,16},{1,3},{3,1},{17,19},{19,17},{4,6},{6,4... | collective-permute-start | bytes 786440 | tf_op jit(solution)/shard_map/ppermute | solution.py:259
  42.7 13.1 %collective-permute-start.3 = (bf16[256,512]{1,0:T(8,128)(2,1)S(1)}, bf16[256,512]{1,0:T(8,128)(2,1)S(1)}, u32[]{:S(2)}, u32[]{:S(2)}) collective-permute-start(bf16[256,512]{1,0:T(8,128)(2,1)S(1)} %get-tuple-element.22), channel_id=1, source_target_pairs={{0,16},{2,18},{16,0},{18,2},{1,17},{3,19},{17,1},{19,3},{4,20},{6,... | collective-permute-start | bytes 786440 | tf_op jit(solution)/shard_map/ppermute | solution.py:259
  44.2 13.2 %collective-permute-start.4 = (bf16[256,512]{1,0:T(8,128)(2,1)S(1)}, bf16[256,512]{1,0:T(8,128)(2,1)S(1)}, u32[]{:S(2)}, u32[]{:S(2)}) collective-permute-start(bf16[256,512]{1,0:T(8,128)(2,1)S(1)} %get-tuple-element.23), channel_id=1, source_target_pairs={{0,18},{2,16},{16,2},{18,0},{1,19},{3,17},{17,3},{19,1},{4,22},{6,... | collective-permute-start | bytes 786440 | tf_op jit(solution)/shard_map/ppermute | solution.py:259
  44.7 24.1 %all-to-all-start.1 = ((bf16[16,48,128]{2,1,0:T(8,128)(2,1)}), bf16[16,48,128]{2,1,0:T(8,128)(2,1)S(1)}, u32[]{:S(2)}, u32[]{:S(2)}) async-start(bf16[16,48,128]{2,1,0:T(8,128)(2,1)} %copy-done), calls=%async_computation.1 | async-start | bytes 393216 | tf_op jit(solution)/shard_map/all_to_all | solution.py:384
  57.6 5.8 %collective-permute-start.5 = (bf16[64,512]{1,0:T(8,128)(2,1)S(1)}, bf16[64,512]{1,0:T(8,128)(2,1)S(1)}, u32[]{:S(2)}, u32[]{:S(2)}) collective-permute-start(bf16[64,512]{1,0:T(8,128)(2,1)S(1)} %get-tuple-element.25), channel_id=1, source_target_pairs={{0,4},{4,0},{8,12},{12,8},{1,5},{5,1},{9,13},{13,9},{2,6},{6,2},{1... | collective-permute-start | bytes 196616 | tf_op jit(solution)/shard_map/ppermute | solution.py:259
  61.0 7.2 %collective-permute-start.6 = (bf16[64,512]{1,0:T(8,128)(2,1)S(1)}, bf16[64,512]{1,0:T(8,128)(2,1)S(1)}, u32[]{:S(2)}, u32[]{:S(2)}) collective-permute-start(bf16[64,512]{1,0:T(8,128)(2,1)S(1)} %get-tuple-element.26), channel_id=1, source_target_pairs={{0,8},{4,12},{8,0},{12,4},{1,9},{5,13},{9,1},{13,5},{2,10},{6,14},... | collective-permute-start | bytes 196616 | tf_op jit(solution)/shard_map/ppermute | solution.py:259
  61.9 6.2 %collective-permute-start.7 = (bf16[64,512]{1,0:T(8,128)(2,1)S(1)}, bf16[64,512]{1,0:T(8,128)(2,1)S(1)}, u32[]{:S(2)}, u32[]{:S(2)}) collective-permute-start(bf16[64,512]{1,0:T(8,128)(2,1)S(1)} %get-tuple-element.27), channel_id=1, source_target_pairs={{0,12},{4,8},{8,4},{12,0},{1,13},{5,9},{9,5},{13,1},{2,14},{6,10},... | collective-permute-start | bytes 196616 | tf_op jit(solution)/shard_map/ppermute | solution.py:259
  68.2 5.0 %collective-permute-start.8 = (f32[64,512]{1,0:T(8,128)S(1)}, f32[64,512]{1,0:T(8,128)S(1)}, u32[]{:S(2)}, u32[]{:S(2)}) collective-permute-start(f32[64,512]{1,0:T(8,128)S(1)} %convert_add_fusion), channel_id=1, source_target_pairs={{0,16},{16,0},{1,17},{17,1},{2,18},{18,2},{3,19},{19,3},{4,20},{20... | collective-permute-start | bytes 393224 | tf_op jit(solution)/shard_map/ppermute | solution.py:376
